TPU v7x, 128 devices: a whole 4x4x4 slice. The times are simulated.
128 devices in a mesh: inp: 8 (over x_lo, z), wt: 4 (over x_hi, core), out: 4 (over y).
Axes of the slice: x: 4 (x_hi: 2, x_lo: 2; x = x_hi * 2 + x_lo), y: 4, z: 4, core: 2. Of those that a mesh axis runs over, the one named last changes fastest.
Arguments:
- tokens: bfloat16 [1024, 8192], P(('wt', 'inp'), 'out'), may hold values from -6 to 6
- out_grad: bfloat16 [1024, 8192], P(('wt', 'inp'), 'out'), may hold values from -1.5 to 1.5
- gate_weight: bfloat16 [8192, 14336], P(('out', 'wt'), 'inp'), may hold values from -0.0625 to 0.0625
- up_weight: bfloat16 [8192, 14336], P(('out', 'wt'), 'inp'), may hold values from -0.0625 to 0.0625
- down_weight: bfloat16 [8192, 14336], P(('out', 'wt'), 'inp'), may hold values from -0.046875 to 0.046875
Outputs:
- input_grad: bfloat16 [1024, 8192], P(('wt', 'inp'), 'out')
- gate_grad: bfloat16 [8192, 14336], P(('out', 'wt'), 'inp')
- up_grad: bfloat16 [8192, 14336], P(('out', 'wt'), 'inp')
- down_grad: bfloat16 [8192, 14336], P(('out', 'wt'), 'inp')
All inputs are finite; a program needn't handle non-finite values.
Results may differ from a plain program's by a relative error of at most 0.03.
Values may be sent and summed in bfloat16 or wider, within the bound.
A program may use at most 128 MiB of HBM per device.

v0:
```python
import jax
import jax.numpy as jnp
from jax import lax
from jax.sharding import PartitionSpec as P


def contract_rows(left, right):
    return lax.dot_general(
        left, right, (((0,), (0,)), ((), ())), preferred_element_type=jnp.float32
    )


def contract_cols(left, right):
    return lax.dot_general(
        left, right, (((1,), (1,)), ((), ())), preferred_element_type=jnp.float32
    )


def activate(gate, up, hidden_grad):
    sigma = jax.nn.sigmoid(gate)
    active = gate * sigma
    hidden = (active * up).astype(jnp.bfloat16)
    up_delta = (hidden_grad * active).astype(jnp.bfloat16)
    gate_delta = (hidden_grad * up * sigma * (1.0 + gate * (1.0 - sigma))).astype(jnp.bfloat16)
    return (hidden, gate_delta, up_delta)


def on_device(tokens, out_grad, gate_weight, up_weight, down_weight):
    token_rows, grad_rows = (
        lax.all_gather(tokens, "inp", axis=0, tiled=True),
        lax.all_gather(out_grad, "inp", axis=0, tiled=True),
    )
    gate_block, up_block, down_block = (
        lax.all_gather(gate_weight, "wt", axis=0, tiled=True),
        lax.all_gather(up_weight, "wt", axis=0, tiled=True),
        lax.all_gather(down_weight, "wt", axis=0, tiled=True),
    )
    gate_part = jnp.dot(token_rows, gate_block, preferred_element_type=jnp.float32)
    up_part = jnp.dot(token_rows, up_block, preferred_element_type=jnp.float32)
    delta_part = jnp.dot(grad_rows, down_block, preferred_element_type=jnp.float32)
    gate_sum, up_sum, delta_sum = (
        lax.psum(gate_part.astype(jnp.bfloat16), "out").astype(jnp.float32),
        lax.psum(up_part.astype(jnp.bfloat16), "out").astype(jnp.float32),
        lax.psum(delta_part.astype(jnp.bfloat16), "out").astype(jnp.float32),
    )
    hidden, gate_delta, up_delta = activate(gate_sum, up_sum, delta_sum)
    input_grad = lax.psum_scatter(
        (contract_cols(gate_delta, gate_block) + contract_cols(up_delta, up_block)).astype(
            jnp.bfloat16
        ),
        "inp",
        scatter_dimension=0,
        tiled=True,
    )
    hidden_cols = hidden.shape[1]
    summed = lax.psum_scatter(
        jnp.concatenate(
            [
                contract_rows(token_rows, gate_delta),
                contract_rows(token_rows, up_delta),
                contract_rows(grad_rows, hidden),
            ],
            axis=1,
        ).astype(jnp.bfloat16),
        "wt",
        scatter_dimension=0,
        tiled=True,
    ).astype(jnp.float32)
    gate_grad = summed[:, :hidden_cols].astype(jnp.bfloat16)
    up_grad = summed[:, hidden_cols : 2 * hidden_cols].astype(jnp.bfloat16)
    down_grad = summed[:, 2 * hidden_cols :].astype(jnp.bfloat16)
    return (input_grad, gate_grad, up_grad, down_grad)


def solution(mesh):
    in_specs = (
        P(("wt", "inp"), "out"),
        P(("wt", "inp"), "out"),
        P(("out", "wt"), "inp"),
        P(("out", "wt"), "inp"),
        P(("out", "wt"), "inp"),
    )
    out_specs = (
        P(("wt", "inp"), "out"),
        P(("out", "wt"), "inp"),
        P(("out", "wt"), "inp"),
        P(("out", "wt"), "inp"),
    )
    return jax.shard_map(
        on_device, mesh=mesh, in_specs=in_specs, out_specs=out_specs, check_vma=False
    )
```

profile of v0, /device:TPU:1, one launch (start us, length us, event | category | flops | bytes accessed | tf_op | source)
XLA Modules:
  0.0 578.9 jit_solution(12294314409452715984)
XLA Ops:
  7.2 0.7 all-gather.10.cloned.1.call-update
  7.9 0.7 all-gather.12.cloned.1.call-update
  10.6 36.7 %all-gather.10.cloned.1.call-done = bf16[256,2048]{1,0:T(8,128)(2,1)} async-done(((bf16[32,2048]{1,0:T(8,128)(2,1)}), bf16[256,2048]{1,0:T(8,128)(2,1)}) %all-gather.10.cloned.1.call-update) | async-done | bytes 1048592 | tf_op jit(solution)/shard_map/all_gather | solution.py:30
  47.2 62.3 %all-gather.12.cloned.1.call-done = bf16[2048,1792]{1,0:T(8,128)(2,1)} async-done(((bf16[512,1792]{1,0:T(8,128)(2,1)}), bf16[2048,1792]{1,0:T(8,128)(2,1)}) %all-gather.12.cloned.1.call-update) | async-done | bytes 7340048 | tf_op jit(solution)/shard_map/all_gather | solution.py:35
  109.6 6.4 %convolution_convert_fusion.4 = bf16[256,1792]{1,0:T(8,128)(2,1)} fusion(bf16[256,2048]{1,0:T(8,128)(2,1)} %all-gather.10.cloned.1.call-done, bf16[2048,1792]{1,0:T(8,128)(2,1)} %all-gather.12.cloned.1.call-done), kind=kOutput, calls=%fused_computation.12 | convolution fusion | flops 1879506944 | bytes 9306112 | tf_op jit(solution)/shard_map/dot_general | solution.py:39
  116.0 51.1 %all-gather.14.cloned.1.call-done = bf16[2048,1792]{1,0:T(8,128)(2,1)} async-done(((bf16[512,1792]{1,0:T(8,128)(2,1)}), bf16[2048,1792]{1,0:T(8,128)(2,1)}) %all-gather.14.cloned.1.call-update) | async-done | bytes 7340048 | tf_op jit(solution)/shard_map/all_gather | solution.py:34
  167.1 6.1 %convolution_convert_fusion.3 = bf16[256,1792]{1,0:T(8,128)(2,1)} fusion(bf16[256,2048]{1,0:T(8,128)(2,1)S(1)} %copy-done, bf16[2048,1792]{1,0:T(8,128)(2,1)} %all-gather.14.cloned.1.call-done), kind=kOutput, calls=%fused_computation.11 | convolution fusion | flops 1879506944 | bytes 9306112 | tf_op jit(solution)/shard_map/dot_general | solution.py:38
  173.2 28.8 %all-gather.6.cloned.1.call-done = bf16[256,2048]{1,0:T(8,128)(2,1)} async-done(((bf16[32,2048]{1,0:T(8,128)(2,1)}), bf16[256,2048]{1,0:T(8,128)(2,1)}) %all-gather.6.cloned.1.call-update) | async-done | bytes 1048592 | tf_op jit(solution)/shard_map/all_gather | solution.py:31
  202.0 62.2 %all-gather.8.cloned.1.call-done = bf16[2048,1792]{1,0:T(8,128)(2,1)} async-done(((bf16[512,1792]{1,0:T(8,128)(2,1)}), bf16[2048,1792]{1,0:T(8,128)(2,1)}) %all-gather.8.cloned.1.call-update) | async-done | bytes 7340048 | tf_op jit(solution)/shard_map/all_gather | solution.py:36
  264.2 6.4 %convolution_convert_fusion.5 = bf16[256,1792]{1,0:T(8,128)(2,1)} fusion(bf16[256,2048]{1,0:T(8,128)(2,1)} %all-gather.6.cloned.1.call-done, bf16[2048,1792]{1,0:T(8,128)(2,1)} %all-gather.8.cloned.1.call-done), kind=kOutput, calls=%fused_computation.13 | convolution fusion | flops 1879506944 | bytes 9306112 | tf_op jit(solution)/shard_map/dot_general | solution.py:40
  270.8 68.7 %all-reduce.3.cloned.1.call-done = (bf16[256,1792]{1,0:T(8,128)(2,1)}, bf16[256,1792]{1,0:T(8,128)(2,1)}, bf16[256,1792]{1,0:T(8,128)(2,1)}) async-done(((bf16[256,1792]{1,0:T(8,128)(2,1)}, bf16[256,1792]{1,0:T(8,128)(2,1)}, bf16[256,1792]{1,0:T(8,128)(2,1)}), (bf16[256,1792]{1,0:T(8,128)(2,1)}, bf16[256,1792]{1,0:T(8,128)(2,1)}, bf16[256,1792]{1,0:T(8,128)(2,1)})) %all-reduce.3.cloned.1.call-update) | async-done | bytes 2752528 | tf_op jit(solution)/shard_map/psum | solution.py:43
  339.5 3.9 fusion.2
  343.5 5.9 %fusion = bf16[2048,1792]{0,1:T(8,128)(2,1)} fusion(bf16[256,2048]{1,0:T(8,128)(2,1)S(1)} %copy-done, bf16[256,1792]{1,0:T(8,128)(2,1)S(1)} %copy-done.6, bf16[256,1792]{1,0:T(8,128)(2,1)S(1)} %copy-done.2, bf16[256,1792]{1,0:T(8,128)(2,1)S(1)} %copy-done.4), kind=kOutput, calls=%fused_computation.4 | convolution fusion | flops 1888681984 | bytes 11141120 | tf_op jit(solution)/shard_map/dot_general | solution.py:8
  349.4 5.3 fusion.1
  354.7 13.5 %pad_maximum_fusion = bf16[2048,5376]{0,1:T(8,128)(2,1)} fusion(bf16[2048,1792]{0,1:T(8,128)(2,1)S(1)} %fusion.2, bf16[2048,1792]{0,1:T(8,128)(2,1)} %fusion.1, bf16[2048,1792]{0,1:T(8,128)(2,1)} %fusion), kind=kLoop, calls=%fused_computation | loop fusion | flops 66060288 | bytes 44040192 | tf_op jit(solution)/shard_map/concatenate | solution.py:57
  368.3 1.1 copy-done.3
  370.0 5.5 fusion.18
  375.5 7.3 %fusion.3 = bf16[256,2048]{1,0:T(8,128)(2,1)} fusion(f32[256,2048]{1,0:T(8,128)S(1)} %fusion.18, bf16[2048,1792]{1,0:T(8,128)(2,1)} %all-gather.12.cloned.1.call-done, bf16[256,1792]{1,0:T(8,128)(2,1)S(1)} %copy-done.3, bf16[256,1792]{1,0:T(8,128)(2,1)S(1)} %copy-done.5), kind=kOutput, calls=%fused_computation.14 | convolution fusion | flops 1883766784 | bytes 12320768 | tf_op jit(solution)/shard_map/dot_general | solution.py:14
  382.8 152.3 %reduce-scatter.5.cloned.1.call-done = bf16[512,5376]{0,1:T(8,128)(2,1)} async-done(((bf16[2048,5376]{0,1:T(8,128)(2,1)}), bf16[512,5376]{0,1:T(8,128)(2,1)}) %reduce-scatter.5.cloned.1.call-update) | async-done | bytes 5505040 | tf_op jit(solution)/shard_map/reduce_scatter | solution.py:56
  535.1 4.8 fusion.20
  539.9 3.8 copy.11
  543.7 3.8 copy.10
  547.5 2.4 copy.9
  549.8 22.2 %reduce-scatter.3.cloned.1.call-done = bf16[32,2048]{1,0:T(8,128)(2,1)} async-done(((bf16[256,2048]{1,0:T(8,128)(2,1)}), bf16[32,2048]{1,0:T(8,128)(2,1)}) %reduce-scatter.3.cloned.1.call-update) | async-done | bytes 131088 | tf_op jit(solution)/shard_map/reduce_scatter | solution.py:47
  (29 shorter events, 2.9 us)
Async XLA Ops:
  7.2 40.1 %all-gather.10.cloned.1.call-start = ((), (), s32[]{:S(2)}) async-start(), calls=%async_computation.4 | async-start | bytes 1179648 | tf_op jit(solution)/shard_map/all_gather | solution.py:30
  7.9 101.7 %all-gather.12.cloned.1.call-start = ((), (), s32[]{:S(2)}) async-start(), calls=%async_computation.5 | async-start | bytes 9175040 | tf_op jit(solution)/shard_map/all_gather | solution.py:35
  8.6 158.4 %all-gather.14.cloned.1.call-start = ((), (), s32[]{:S(2)}) async-start(), calls=%async_computation.6 | async-start | bytes 9175040 | tf_op jit(solution)/shard_map/all_gather | solution.py:34
  9.4 192.6 %all-gather.6.cloned.1.call-start = ((), (), s32[]{:S(2)}) async-start(), calls=%async_computation.2 | async-start | bytes 1179648 | tf_op jit(solution)/shard_map/all_gather | solution.py:31
  10.0 254.2 %all-gather.8.cloned.1.call-start = ((), (), s32[]{:S(2)}) async-start(), calls=%async_computation.3 | async-start | bytes 9175040 | tf_op jit(solution)/shard_map/all_gather | solution.py:36
  10.5 329.0 %all-reduce.3.cloned.1.call-start = ((), (), s32[]{:S(2)}) async-start(), calls=%async_computation.9 | async-start | bytes 5505024 | tf_op jit(solution)/shard_map/psum | solution.py:43
  47.2 119.8 %copy-start = (bf16[256,2048]{1,0:T(8,128)(2,1)S(1)}, bf16[256,2048]{1,0:T(8,128)(2,1)}, u32[]{:S(2)}) copy-start(bf16[256,2048]{1,0:T(8,128)(2,1)} %all-gather.10.cloned.1.call-done) | copy-start | bytes 3145732
  270.6 68.9 %copy-start.1 = (bf16[256,2048]{1,0:T(8,128)(2,1)S(1)}, bf16[256,2048]{1,0:T(8,128)(2,1)}, u32[]{:S(2)}) copy-start(bf16[256,2048]{1,0:T(8,128)(2,1)} %all-gather.6.cloned.1.call-done) | copy-start | bytes 3145732
  270.6 264.5 %reduce-scatter.5.cloned.1.call-start = ((), (), s32[]{:S(2)}) async-start(), calls=%async_computation.8 | async-start | bytes 27525120 | tf_op jit(solution)/shard_map/reduce_scatter | solution.py:56
  339.5 4.0 copy-start.2
  339.5 4.0 copy-start.4
  339.5 4.0 copy-start.6
  368.2 1.2 copy-start.3
  368.2 1.4 copy-start.5
  368.2 1.7 copy-start.7
  368.3 203.8 %reduce-scatter.3.cloned.1.call-start = ((), (), s32[]{:S(2)}) async-start(), calls=%async_computation.7 | async-start | bytes 1179648 | tf_op jit(solution)/shard_map/reduce_scatter | solution.py:47
Sparse Core Ops, SparseCore 0:
  9.6 37.5 all-gather.9
  48.9 60.6 all-gather.11
  111.2 55.7 all-gather.13
  168.6 33.3 all-gather.5
  203.5 60.6 all-gather.7
  270.7 68.7 all-reduce.2
  368.4 166.6 reduce-scatter.4
  538.1 33.8 reduce-scatter.2
where the time goes:
time: 583 us; the launch traced here: 579 us
  waiting for transfers between devices  487 us (84%)
  matrix products  46.8 us (8%)
  local copies, waits for them, and re-layouts  16.4 us (3%)
  between operations  14.2 us (2%)
  other arithmetic  13.5 us (2%)
    reduce_scatter x1, waiting for transfers between devices, on_device(): lax.psum_scatter(jnp.concatenate([contract_rows(token_rows, gate_delta),...  152 us
    psum x1, waiting for transfers between devices, on_device(): lax.psum(up_part.astype(jnp.bfloat16), 'out').astype(jnp.float32)  68.7 us
    all_gather x1, waiting for transfers between devices, on_device(): lax.all_gather(up_weight, 'wt', axis=0, tiled=True)  62.3 us
    all_gather x1, waiting for transfers between devices, on_device(): lax.all_gather(down_weight, 'wt', axis=0, tiled=True)  62.2 us
    all_gather x1, waiting for transfers between devices, on_device(): lax.all_gather(gate_weight, 'wt', axis=0, tiled=True)  51.1 us
    all_gather x1, waiting for transfers between devices, on_device(): lax.all_gather(tokens, 'inp', axis=0, tiled=True)  36.7 us
    all_gather x1, waiting for transfers between devices, on_device(): lax.all_gather(out_grad, 'inp', axis=0, tiled=True)  28.8 us
    reduce_scatter x1, waiting for transfers between devices, on_device(): lax.psum_scatter((contract_cols(gate_delta, gate_block) + contract_cols(u...  22.2 us
  transfers between devices with their start and end apart: 8, of which 8 were waited for; matrix products, arithmetic and copies ran while one was open for 7% of the time, Pallas kernels for 0%

commit v1 on v0

v1 whole, which is shorter than its diff:
```python
import functools

import jax
import jax.numpy as jnp
from jax import lax
from jax.experimental import pallas as pl
from jax.experimental.pallas import tpu as pltpu
from jax.sharding import PartitionSpec as P

BF16 = jnp.bfloat16
F32 = jnp.float32
MESH = pl.DeviceIdType.MESH
N_SEM = 208

ORDER = (
    ("T1", 0), ("T1", 1), ("F", 0), ("TR", 0), ("A1", 0), ("T2", 0), ("F", 1), ("F", 2), ("B1", 0), ("A2", 0),
    ("TR", 1), ("T3", 0), ("A1", 1), ("TR", 2), ("F", 3), ("B1", 1), ("A1", 2), ("TR", 3), ("B2", 0), ("A2", 1),
    ("B1", 2), ("A1", 3), ("A3", 0), ("B2", 1), ("A2", 2), ("B3", 0), ("B1", 3), ("B2", 2), ("A3", 1), ("A3s", 1),
    ("A2", 3), ("A3", 2), ("B3", 1), ("B2", 3), ("B3s", 1), ("A3s", 2), ("B3", 2), ("A4", 1), ("B3s", 2), ("A3", 3),
    ("B3", 3), ("A3s", 3), ("B3s", 3), ("A3s", 0), ("B3s", 0), ("B4", 1), ("A4", 2), ("A5", 1), ("A4", 3), ("B4", 2),
    ("A4", 0), ("B4", 3), ("B4", 0), ("B5", 1), ("A5", 2), ("A5", 3), ("B5", 2), ("A5", 0), ("B5", 3), ("B5", 0),
    ("C", 1), ("G", 1), ("C", 2), ("C", 3), ("G", 2), ("I3", 0), ("I12", 0), ("G", 3), ("C", 0), ("I12b", 0),
    ("I0", 0), ("G", 0), ("I0f", 0),
)


def kernel(
    tok_in, og_in, wg_in, wu_in, wd_in, ig_out, gg_out, ug_out, dg_out,
    w, tok, ttr, pp, pq, r1p, r1q, r2p, r2q, rxp, rxq, dp, dq, acc, go, ig, rigc, rz1, rz2, rix, igo,
    ssem, rsem, lsem,
):
    inp, wt, y = lax.axis_index("inp"), lax.axis_index("wt"), lax.axis_index("out")
    xl, z, xh, c = inp // 4, inp % 4, wt // 2, wt % 2
    yn, yp, yo = (y + 1) % 4, (y + 3) % 4, (y + 2) % 4
    oxh, oxl, oc = 1 - xh, 1 - xl, 1 - c
    core = {"wt": xh * 2 + oc}
    x2 = {"wt": oxh * 2 + c}
    xlp = {"inp": oxl * 4 + z}
    diag = {"inp": oxl * 4 + z, "wt": oxh * 2 + c}
    zn, zp = {"inp": xl * 4 + (z + 1) % 4}, {"inp": xl * 4 + (z + 3) % 4}
    ynd, ypd = {"out": yn}, {"out": yp}
    feats, half = w.shape[1], w.shape[2]
    own_f = feats // 2
    p_cols, q_cols = pp.shape[-1], pq.shape[-1]
    rows = tok.shape[-2]
    chunk = 8 * rows
    hr = rows // 2
    cols = lambda h: pl.ds(pl.multiple_of(h * feats, 128), feats)
    hcols = lambda h: pl.ds(pl.multiple_of(h * half, 128), half)
    frows = lambda h: pl.ds(pl.multiple_of(h * own_f, 16), own_f)

    arrivals, all_sends = {}, []

    def send(name, src, dst, device):
        i = len(all_sends)
        assert i < N_SEM
        cp = pltpu.make_async_remote_copy(
            src_ref=src, dst_ref=dst, send_sem=ssem.at[i], recv_sem=rsem.at[i], device_id=device, device_id_type=MESH
        )
        cp.start()
        all_sends.append(cp)
        arrivals[name] = cp

    def arrive(*name):
        arrivals.pop(name).wait_recv()

    local = []

    def bring(src, dst):
        cp = pltpu.make_async_copy(src, dst, lsem.at[len(local)])
        cp.start()
        local.append(cp)

    acts = (tok_in, og_in)
    weights = (wg_in, wu_in, wd_in)
    for a in (0, 1):
        bring(acts[a].at[:, cols(xh)], tok.at[0, xh, c, xl, a])
    for a in range(3):
        bring(weights[a].at[:, hcols(c)], w.at[a, frows(c), :])

    barrier = pltpu.get_barrier_semaphore()
    for device in (core, x2, xlp, diag, zn, zp, ynd, ypd):
        pl.semaphore_signal(barrier, inc=1, device_id=device, device_id_type=MESH)
    pl.semaphore_wait(barrier, 8)

    near = (("xlp", xlp, xh, xh, oxl), ("diag", diag, oxh, oxh, oxl), ("x2", x2, oxh, oxh, xl))
    for a in (0, 1):
        for name, device, h, _, _ in near:
            send(("x0", name, a), acts[a].at[:, cols(h)], tok.at[0, xh, c, xl, a], device)
    for a in (0, 1):
        mine = acts[a].at[:, cols(xh)]
        send(("c0", "own", a), mine, tok.at[0, xh, c, xl, a], core)
    for a in range(3):
        send(("w", a), weights[a].at[:, hcols(oc)], w.at[a, frows(c), :], core)
    for a in (0, 1):
        mine = acts[a].at[:, cols(xh)]
        send(("zn", "own", a), mine, tok.at[2, xh, c, xl, a], zn)
        send(("zp", "own", a), mine, tok.at[1, xh, c, xl, a], zp)

    def T1(a):
        for name, _, _, sxh, sxl in near:
            arrive("x0", name, a)
            block = tok.at[0, sxh, c, sxl, a]
            send(("c0", name, a), block, block, core)
            send(("zn", name, a), block, tok.at[2, sxh, c, sxl, a], zn)
            send(("zp", name, a), block, tok.at[1, sxh, c, sxl, a], zp)

    def T2(_):
        for way in ("zn", "zp"):
            for name in ("own", "xlp", "diag", "x2"):
                for a in (0, 1):
                    arrive(way, name, a)
        send(("zf", 0), tok.at[2, 0, c], tok.at[3, 0, c], zn)
        send(("zf", 1), tok.at[1, 1, c], tok.at[3, 1, c], zp)
        for k in (1, 2):
            send(("ck", k), tok.at[k, :, c], tok.at[k, :, c], core)

    def T3(_):
        for h in (0, 1):
            arrive("zf", h)
            send(("ck3", h), tok.at[3, h, c], tok.at[3, h, c], core)

    def project(k, a):
        left = tok[k, :, :, :, a // 2].reshape(chunk, feats)
        pp[k, :, :, a] = jnp.dot(left, w[a, :, :p_cols], preferred_element_type=F32).astype(BF16).reshape(4, 2, rows, p_cols)
        pq[k, :, :, a] = jnp.dot(left, w[a, :, p_cols:], preferred_element_type=F32).astype(BF16).reshape(4, 2, rows, q_cols)

    def F(k):
        if k == 0:
            for a in (0, 1):
                local[a].wait()
                for name in ("own", "xlp", "diag", "x2"):
                    arrive("c0", name, a)
            for a in range(3):
                local[2 + a].wait()
                arrive("w", a)
        elif k == 3:
            arrive("ck3", 0)
            arrive("ck3", 1)
        else:
            arrive("ck", k)

        @pl.loop(0, 3)
        def _(a):
            project(k, a)

        send(("s1", k, 0), pp.at[k, yo, 0], r1p.at[k, 0], ynd)
        send(("s1", k, 1), pp.at[k, yo, 1], r1p.at[k, 1], ypd)
        for j, t in enumerate((yo, yn, yp, y)):
            send(("qx", k, j), pq.at[k, t, oxh], rxq.at[k, t], x2)
        send(("s2", k, 0, 1), pp.at[k, yn, 1], r2p.at[k, 0, 1], ynd)
        send(("s2", k, 1, 0), pp.at[k, yp, 0], r2p.at[k, 1, 0], ypd)

    def add(ref, *others):
        total = ref[...].astype(F32)
        for other in others:
            total += other[...].astype(F32)
        return total

    def A1(k):
        for way, t, device in ((0, yn, ynd), (1, yp, ypd)):
            arrive("s1", k, way)
            ref = pp.at[k, t, way]
            ref[...] = add(ref, r1p.at[k, way]).astype(BF16)
            send(("s2", k, way, way), ref, r2p.at[k, way, way], device)

    def B1(k):
        for j, t in enumerate((yo, yn, yp, y)):
            arrive("qx", k, j)
            ref = pq.at[k, t, xh]
            ref[...] = add(ref, rxq.at[k, t]).astype(BF16)
            if j == 0:
                send(("t1", k, 0), ref.at[:, :hr], r1q.at[k, 0], ynd)
                send(("t1", k, 1), ref.at[:, hr:], r1q.at[k, 1], ypd)
            if j == 1:
                send(("t2", k, 0, 1), ref.at[:, hr:], r2q.at[k, 0, :, hr:], ynd)
            if j == 2:
                send(("t2", k, 1, 0), ref.at[:, :hr], r2q.at[k, 1, :, :hr], ypd)

    def B2(k):
        for way, t, device in ((0, yn, ynd), (1, yp, ypd)):
            arrive("t1", k, way)
            part = slice(0, hr) if way == 0 else slice(hr, rows)
            ref = pq.at[k, t, xh, :, part]
            ref[...] = add(ref, r1q.at[k, way]).astype(BF16)
            send(("t2", k, way, way), ref, r2q.at[k, way, :, part], device)

    def A2(k):
        for way in (0, 1):
            for h in (0, 1):
                arrive("s2", k, way, h)
        ref = pp.at[k, y, oxh]
        ref[...] = add(ref, r2p.at[k, 0, oxh], r2p.at[k, 1, oxh]).astype(BF16)
        send(("rx", k), ref, rxp.at[k], x2)

    def activate(sums, out):
        gate, up, hidden_grad = sums[0], sums[1], sums[2]
        sigma = jax.nn.sigmoid(gate)
        active = gate * sigma
        out[0] = (hidden_grad * up * sigma * (1.0 + gate * (1.0 - sigma))).astype(BF16)
        out[1] = (hidden_grad * active).astype(BF16)
        out[2] = (active * up).astype(BF16)

    def A3(k):
        arrive("rx", k)
        activate(add(pp.at[k, y, xh], r2p.at[k, 0, xh], r2p.at[k, 1, xh], rxp.at[k]), dp.at[k, y, xh])

    def A3s(k):
        ref = dp.at[k, y, xh]
        send(("dx", k), ref, ref, x2)
        send(("do", k, 0), ref, ref, ynd)
        send(("do", k, 1), ref, ref, ypd)

    def B3(k):
        for way in (0, 1):
            for h in (0, 1):
                arrive("t2", k, way, h)
        activate(add(pq.at[k, y, xh], r2q.at[k, 0], r2q.at[k, 1]), dq.at[k, y, xh])

    def B3s(k):
        ref = dq.at[k, y, xh]
        send(("eo", k, 0), ref, ref, ynd)
        send(("eo", k, 1), ref, ref, ypd)
        send(("ex", k, 0), ref, ref, x2)

    def A4(k):
        arrive("dx", k)
        ref = dp.at[k, y, oxh]
        send(("dt", k, 0), ref, ref, ynd)
        send(("dt", k, 1), ref, ref, ypd)

    def A5(k):
        arrive("do", k, 0)
        ref = dp.at[k, yp, xh]
        send(("df", k, 0), ref, ref, ynd)
        arrive("dt", k, 1)
        ref = dp.at[k, yn, oxh]
        send(("df", k, 1), ref, ref, ypd)

    def B4(k):
        arrive("eo", k, 0)
        ref = dq.at[k, yp, xh, :, :hr]
        send(("ef", k, 0), ref, ref, ynd)
        arrive("eo", k, 1)
        ref = dq.at[k, yn, xh, :, hr:]
        send(("ef", k, 1), ref, ref, ypd)
        for j, t in ((1, yp), (2, yn)):
            ref = dq.at[k, t, xh]
            send(("ex", k, j), ref, ref, x2)

    def B5(k):
        arrive("ef", k, 0)
        arrive("ef", k, 1)
        ref = dq.at[k, yo, xh]
        send(("ex", k, 3), ref, ref, x2)

    def TR(k):
        @pl.loop(0, 2)
        def _(a):
            ttr[a, k] = tok[k, :, :, :, a].reshape(chunk, feats).T

    def C(k):
        for name in (("df", k, 0), ("df", k, 1), ("dt", k, 0), ("do", k, 1), ("ex", k, 0), ("ex", k, 1), ("ex", k, 2), ("ex", k, 3)):
            arrive(*name)
        nt = (((1,), (1,)), ((), ()))

        @pl.loop(0, 2)
        def _(j):
            fr = pl.ds(pl.multiple_of(j * own_f, 128), own_f)
            total = jnp.zeros((chunk, own_f), F32)
            for a in (0, 1):
                left = dp[k, :, :, a].reshape(chunk, p_cols)
                total += lax.dot_general(left, w[a, fr, :p_cols], nt, preferred_element_type=F32)
                left = dq[k, :, :, a].reshape(chunk, q_cols)
                total += lax.dot_general(left, w[a, fr, p_cols:], nt, preferred_element_type=F32)
            ig[k, :, :, :, :, fr] = total.astype(BF16).reshape(2, 2, 2, rows, own_f)

        send(("igc", k), ig.at[k, :, oc], rigc.at[k], core)

    def gradient(k, a, part, first, last):
        left = ttr[a // 2, k, part, :]
        for ref, lanes in ((dp, slice(0, p_cols)), (dq, slice(p_cols, half))):
            right = ref[k, :, :, a].reshape(chunk, ref.shape[-1])
            value = jnp.dot(left, right, preferred_element_type=F32)
            if not first:
                value += acc[a, part, lanes]
            if last:
                go[a, part, lanes] = value.astype(BF16)
            else:
                acc[a, part, lanes] = value

    outs = (gg_out, ug_out, dg_out)

    def G(k):
        first, last = k == 1, k == 0
        if not last:
            @pl.loop(0, 6)
            def _(i):
                gradient(k, i // 2, pl.ds(pl.multiple_of((i % 2) * own_f, 128), own_f), first, last)
        else:
            for h, remote in ((oc, True), (c, False)):
                for a in range(3):
                    gradient(k, a, frows(h), first, last)
                    if remote:
                        send(("go", a), go.at[a, frows(h), :], outs[a].at[:, hcols(c)], core)
                    else:
                        bring(go.at[a, frows(h), :], outs[a].at[:, hcols(c)])

    def both(k, h):
        return ig[k, h, c].astype(F32) + rigc[k, h].astype(F32)

    def I3(_):
        arrive("igc", 3)
        for h in (0, 1):
            ref = ig.at[3, h, c]
            ref[...] = both(3, h).astype(BF16)
            send(("z1", h), ref, rz1.at[h], zn if h == 0 else zp)

    def I12(_):
        for k, device, way in ((1, zn, 0), (2, zp, 1)):
            arrive("igc", k)
            h = 1 - way
            ref = ig.at[k, h, c]
            ref[...] = both(k, h).astype(BF16)
            send(("z2", way, h), ref, rz2.at[way, h], device)

    def I12b(_):
        for k, device, way in ((1, zn, 0), (2, zp, 1)):
            arrive("z1", way)
            ref = ig.at[k, way, c]
            ref[...] = (both(k, way) + rz1[way].astype(F32)).astype(BF16)
            send(("z2", way, way), ref, rz2.at[way, way], device)

    def I0(_):
        arrive("igc", 0)
        for h in (0, 1):
            for way in (0, 1):
                arrive("z2", way, h)
            ig[0, h, c] = (both(0, h) + rz2[0, h].astype(F32) + rz2[1, h].astype(F32)).astype(BF16)
        send(("ix", 0), ig.at[0, xh, c, oxl], rix.at[0], xlp)
        send(("ix", 1), ig.at[0, oxh, c, oxl], rix.at[1], diag)
        send(("ix", 2), ig.at[0, oxh, c, xl], rix.at[2], x2)

    def I0f(_):
        for j in range(3):
            arrive("ix", j)
        igo[:, cols(xh)] = (ig[0, xh, c, xl].astype(F32) + rix[0].astype(F32)).astype(BF16)
        igo[:, cols(oxh)] = (rix[1].astype(F32) + rix[2].astype(F32)).astype(BF16)
        bring(igo, ig_out)

    steps = dict(
        T1=T1, T2=T2, T3=T3, F=F, A1=A1, B1=B1, B2=B2, A2=A2, A3=A3, A3s=A3s, B3=B3, B3s=B3s, A4=A4, A5=A5, B4=B4,
        B5=B5, TR=TR, C=C, G=G, I3=I3, I12=I12, I12b=I12b, I0=I0, I0f=I0f,
    )
    for step, k in ORDER:
        steps[step](k)
    for a in range(3):
        arrive("go", a)
    for cp in local[5:]:
        cp.wait()
    for cp in all_sends:
        cp.wait_send()
    assert not arrivals, "left over"


def on_device(tokens, out_grad, gate_weight, up_weight, down_weight):
    rows, model = tokens.shape
    own_f, hidden = gate_weight.shape
    feats, half = 2 * own_f, hidden // 2
    q_cols = (half // 128 * 3 // 7) * 128
    p_cols = half - q_cols
    hr = rows // 2
    vmem = lambda *shape: pltpu.VMEM(shape, BF16)
    any_spec = pl.BlockSpec(memory_space=pl.ANY)
    out_shapes = [tokens, gate_weight, up_weight, down_weight]
    return pl.pallas_call(
        kernel,
        out_shape=[jax.ShapeDtypeStruct(o.shape, BF16) for o in out_shapes],
        in_specs=[any_spec] * 5,
        out_specs=[any_spec] * 4,
        scratch_shapes=[
            vmem(3, feats, half),
            vmem(4, 2, 2, 2, 2, rows, feats),
            vmem(2, 4, feats, 8 * rows),
            vmem(4, 4, 2, 3, rows, p_cols),
            vmem(4, 4, 2, 3, rows, q_cols),
            vmem(4, 2, 3, rows, p_cols),
            vmem(4, 2, 3, hr, q_cols),
            vmem(4, 2, 2, 3, rows, p_cols),
            vmem(4, 2, 3, rows, q_cols),
            vmem(4, 3, rows, p_cols),
            vmem(4, 4, 3, rows, q_cols),
            vmem(4, 4, 2, 3, rows, p_cols),
            vmem(4, 4, 2, 3, rows, q_cols),
            pltpu.VMEM((3, feats, half), F32),
            vmem(3, feats, half),
            vmem(4, 2, 2, 2, rows, feats),
            vmem(4, 2, 2, rows, feats),
            vmem(2, 2, rows, feats),
            vmem(2, 2, 2, rows, feats),
            vmem(3, rows, feats),
            vmem(rows, model),
            pltpu.SemaphoreType.DMA((N_SEM,)),
            pltpu.SemaphoreType.DMA((N_SEM,)),
            pltpu.SemaphoreType.DMA((16,)),
        ],
        compiler_params=pltpu.CompilerParams(
            collective_id=0, has_side_effects=True, vmem_limit_bytes=60 * 2**20
        ),
        cost_estimate=pl.CostEstimate(flops=15 * 10**9, bytes_accessed=12 * 2**20, transcendentals=10**6),
    )(tokens, out_grad, gate_weight, up_weight, down_weight)


def solution(mesh):
    in_specs = (
        P(("wt", "inp"), "out"),
        P(("wt", "inp"), "out"),
        P(("out", "wt"), "inp"),
        P(("out", "wt"), "inp"),
        P(("out", "wt"), "inp"),
    )
    out_specs = (
        P(("wt", "inp"), "out"),
        P(("out", "wt"), "inp"),
        P(("out", "wt"), "inp"),
        P(("out", "wt"), "inp"),
    )
    return jax.shard_map(
        on_device, mesh=mesh, in_specs=in_specs, out_specs=out_specs, check_vma=False
    )
```

time: 583 us -> 126 us (0.22)
  waiting for transfers between devices: 487 us -> 0 us
  Pallas kernels: 0 us -> 117 us
  matrix products: 46.8 us -> 0 us
  between operations: 14.2 us -> 0.64 us
  other arithmetic: 13.5 us -> 0 us
  local copies, waits for them, and re-layouts: 16.4 us -> 7.94 us
    all_gather x5 -> x0, waiting for transfers between devices: 241 us -> none  [the longest x1 62.3 us: on_device(): lax.all_gather(up_weight, 'wt', axis=0, tiled=True)]
    reduce_scatter x2 -> x0, waiting for transfers between devices: 174 us -> none  [the longest x1 152 us: on_device(): lax.psum_scatter(jnp.concatenate([contract_rows(token_rows, gate_delta),...]
    pallas_call x0 -> x1, Pallas kernels: none -> 117 us  [on_device(): pl.pallas_call(kernel, out_shape=[jax.ShapeDtypeStruct(o.shape, BF16) for...]
    psum x1 -> x0, waiting for transfers between devices: 68.7 us -> none  [on_device(): lax.psum(up_part.astype(jnp.bfloat16), 'out').astype(jnp.float32)]
    dot_general x8 -> x0, matrix products: 46.8 us -> none  [the longest x3 15.1 us: contract_rows(): lax.dot_general(left, right, (((0,), (0,)), ((), ())), preferred_element_...]
    concatenate x1 -> x0, other arithmetic: 13.5 us -> none  [on_device(): jnp.concatenate([contract_rows(token_rows, gate_delta), contract_rows(tok...]
  transfers between devices with their start and end apart: 8 -> 0, of which waited for: 8 -> 0; matrix products, arithmetic and copies ran while one was open for 7% -> 0% of each run, Pallas kernels for 0% -> 0%
where the time goes in v1:
time: 126 us
  Pallas kernels  117 us (93%)
  local copies, waits for them, and re-layouts  7.94 us (6%)
    pallas_call x1, Pallas kernels, on_device(): pl.pallas_call(kernel, out_shape=[jax.ShapeDtypeStruct(o.shape, BF16) for...  117 us
    unnamed x8, local copies, waits for them, and re-layouts  7.94 us

profile of v1, /device:TPU:1, one launch (start us, length us, event | category | flops | bytes accessed | tf_op | source)
XLA Modules:
  0.0 125.7 jit_solution(12469252792220879858)
XLA Ops:
  0.6 117.1 %shard_map.84 = (bf16[32,2048]{1,0:T(8,128)(2,1)}, bf16[512,1792]{1,0:T(8,128)(2,1)}, bf16[512,1792]{1,0:T(8,128)(2,1)}, bf16[512,1792]{1,0:T(8,128)(2,1)}) custom-call(bf16[32,2048]{1,0:T(8,128)(2,1)} %tok_in.1, bf16[32,2048]{1,0:T(8,128)(2,1)} %og_in.1, bf16[512,1792]{1,0:T(8,128)(2,1)} %wg_in.1, bf16[512,1792]{1,0:T(8,128)(2,1)} %wu_in.1, ...), custom_call_target="tpu_custom_call" | custom-call | flops 15000000512 | bytes 12582912 | tf_op jit(solution)/shard_map/pallas_call | solution.py:376
  117.8 1.6 %copy.13 = bf16[32,2048]{1,0:T(8,128)(2,1)} copy(bf16[32,2048]{1,0:T(8,128)(2,1)} %get-tuple-element.8) | data formatting | bytes 262144
  119.4 0.0 copy-start.1
  119.4 3.0 %copy.14 = bf16[512,1792]{1,0:T(8,128)(2,1)} copy(bf16[512,1792]{1,0:T(8,128)(2,1)} %get-tuple-element.9) | data formatting | bytes 3670016
  122.3 0.0 copy-done.1
  122.3 0.0 copy-start
  122.3 1.2 copy.15
  123.6 0.9 copy-done
  124.5 1.2 copy.16
Async XLA Ops:
  119.4 3.0 %copy-start.1 = (bf16[512,1792]{1,0:T(8,128)(2,1)S(1)}, bf16[512,1792]{1,0:T(8,128)(2,1)}, u32[]{:S(2)}) copy-start(bf16[512,1792]{1,0:T(8,128)(2,1)} %get-tuple-element.10) | copy-start | bytes 5505028
  122.3 2.2 %copy-start = (bf16[512,1792]{1,0:T(8,128)(2,1)S(1)}, bf16[512,1792]{1,0:T(8,128)(2,1)}, u32[]{:S(2)}) copy-start(bf16[512,1792]{1,0:T(8,128)(2,1)} %get-tuple-element.11) | copy-start | bytes 5505028

commit v2 on v1

--- a/solution.py
+++ b/solution.py
@@ -13,20 +13,22 @@
 N_SEM = 208
 
 ORDER = (
-    ("T1", 0), ("T1", 1), ("F", 0), ("TR", 0), ("A1", 0), ("T2", 0), ("F", 1), ("F", 2), ("B1", 0), ("A2", 0),
-    ("TR", 1), ("T3", 0), ("A1", 1), ("TR", 2), ("F", 3), ("B1", 1), ("A1", 2), ("TR", 3), ("B2", 0), ("A2", 1),
-    ("B1", 2), ("A1", 3), ("A3", 0), ("B2", 1), ("A2", 2), ("B3", 0), ("B1", 3), ("B2", 2), ("A3", 1), ("A3s", 1),
-    ("A2", 3), ("A3", 2), ("B3", 1), ("B2", 3), ("B3s", 1), ("A3s", 2), ("B3", 2), ("A4", 1), ("B3s", 2), ("A3", 3),
-    ("B3", 3), ("A3s", 3), ("B3s", 3), ("A3s", 0), ("B3s", 0), ("B4", 1), ("A4", 2), ("A5", 1), ("A4", 3), ("B4", 2),
-    ("A4", 0), ("B4", 3), ("B4", 0), ("B5", 1), ("A5", 2), ("A5", 3), ("B5", 2), ("A5", 0), ("B5", 3), ("B5", 0),
-    ("C", 1), ("G", 1), ("C", 2), ("C", 3), ("G", 2), ("I3", 0), ("I12", 0), ("G", 3), ("C", 0), ("I12b", 0),
-    ("I0", 0), ("G", 0), ("I0f", 0),
+    ("T1", 0), ("F", 0, 0), ("T1", 1), ("F", 0, 1), ("A1", 0), ("T2", 0), ("B1a", 0), ("B1b", 0), ("F", 1),
+    ("F", 2), ("A1", 1), ("T3", 0), ("B1a", 1), ("F", 3), ("A2", 1), ("B1b", 1), ("B2", 1), ("B1a", 2), ("A1", 3),
+    ("B1b", 2), ("B2", 2), ("A2", 0), ("A1", 2), ("B2", 0), ("B3", 1), ("A2", 3), ("B1a", 3), ("B3y", 1),
+    ("B1b", 3), ("A3", 1), ("A3x", 1), ("A2", 2), ("B2", 3), ("B3x", 1), ("A3", 0), ("A3y", 1), ("A3", 3),
+    ("A3y", 3), ("B3", 2), ("A3x", 3), ("B4y", 1), ("B3", 3), ("A3", 2), ("B4x", 1), ("B3x", 3), ("B3y", 2),
+    ("A4", 1), ("B3y", 3), ("A4", 3), ("B5", 1), ("A5b", 1), ("B4y", 2), ("A3x", 2), ("A5a", 1), ("B4x", 2),
+    ("B4y", 3), ("A3y", 2), ("B4x", 3), ("A4", 2), ("A5a", 3), ("B5", 3), ("A3x", 0), ("B3", 0), ("A5b", 3),
+    ("B5", 2), ("B3y", 0), ("C", 1), ("B3x", 2), ("B3x", 0), ("G", 1), ("A5b", 2), ("A5a", 2), ("A3y", 0), ("C", 3),
+    ("B4y", 0), ("A4", 0), ("G", 3), ("I3", 0), ("B4x", 0), ("C", 2), ("A5a", 0), ("I12", 0), ("B5", 0), ("A5b", 0),
+    ("I12b", 0), ("G", 2), ("C", 0), ("I0", 0), ("G", 0), ("I0f", 0),
 )
 
 
 def kernel(
     tok_in, og_in, wg_in, wu_in, wd_in, ig_out, gg_out, ug_out, dg_out,
-    w, tok, ttr, pp, pq, r1p, r1q, r2p, r2q, rxp, rxq, dp, dq, acc, go, ig, rigc, rz1, rz2, rix, igo,
+    w, tok, ttr, pp, pq, r1p, r1q, r2p, r2q, rxp, rxq, dp, dq, acc, go, ig, rigc, rz1, rz2, rix,
     ssem, rsem, lsem,
 ):
     inp, wt, y = lax.axis_index("inp"), lax.axis_index("wt"), lax.axis_index("out")
@@ -72,6 +74,7 @@
         local.append(cp)
 
     acts = (tok_in, og_in)
+    outs = (gg_out, ug_out, dg_out)
     weights = (wg_in, wu_in, wd_in)
     for a in (0, 1):
         bring(acts[a].at[:, cols(xh)], tok.at[0, xh, c, xl, a])
@@ -125,13 +128,16 @@
         pp[k, :, :, a] = jnp.dot(left, w[a, :, :p_cols], preferred_element_type=F32).astype(BF16).reshape(4, 2, rows, p_cols)
         pq[k, :, :, a] = jnp.dot(left, w[a, :, p_cols:], preferred_element_type=F32).astype(BF16).reshape(4, 2, rows, q_cols)
 
-    def F(k):
+    def groups(k):
+        return ((0, 2), (2, 3)) if k == 0 else ((0, 3),)
+
+    def F(k, g=0):
+        first, last = groups(k)[g]
         if k == 0:
-            for a in (0, 1):
-                local[a].wait()
-                for name in ("own", "xlp", "diag", "x2"):
-                    arrive("c0", name, a)
-            for a in range(3):
+            local[g].wait()
+            for name in ("own", "xlp", "diag", "x2"):
+                arrive("c0", name, g)
+            for a in range(first, last):
                 local[2 + a].wait()
                 arrive("w", a)
         elif k == 3:
@@ -140,16 +146,21 @@
         else:
             arrive("ck", k)
 
-        @pl.loop(0, 3)
+        @pl.loop(first, last)
         def _(a):
             project(k, a)
 
-        send(("s1", k, 0), pp.at[k, yo, 0], r1p.at[k, 0], ynd)
-        send(("s1", k, 1), pp.at[k, yo, 1], r1p.at[k, 1], ypd)
+        part = slice(first, last)
+        send(("s1", k, 0, g), pp.at[k, yo, 0, part], r1p.at[k, 0, part], ynd)
+        send(("s1", k, 1, g), pp.at[k, yo, 1, part], r1p.at[k, 1, part], ypd)
         for j, t in enumerate((yo, yn, yp, y)):
-            send(("qx", k, j), pq.at[k, t, oxh], rxq.at[k, t], x2)
-        send(("s2", k, 0, 1), pp.at[k, yn, 1], r2p.at[k, 0, 1], ynd)
-        send(("s2", k, 1, 0), pp.at[k, yp, 0], r2p.at[k, 1, 0], ypd)
+            send(("qx", k, j, g), pq.at[k, t, oxh, part], rxq.at[k, t, part], x2)
+        send(("s2i", k, 0, g), pp.at[k, yn, 1, part], r2p.at[k, 0, 1, part], ynd)
+        send(("s2i", k, 1, g), pp.at[k, yp, 0, part], r2p.at[k, 1, 0, part], ypd)
+
+    def arrive_groups(k, *name):
+        for g in range(len(groups(k))):
+            arrive(*name, g)
 
     def add(ref, *others):
         total = ref[...].astype(F32)
@@ -159,23 +170,27 @@
 
     def A1(k):
         for way, t, device in ((0, yn, ynd), (1, yp, ypd)):
-            arrive("s1", k, way)
+            arrive_groups(k, "s1", k, way)
             ref = pp.at[k, t, way]
             ref[...] = add(ref, r1p.at[k, way]).astype(BF16)
-            send(("s2", k, way, way), ref, r2p.at[k, way, way], device)
-
-    def B1(k):
-        for j, t in enumerate((yo, yn, yp, y)):
-            arrive("qx", k, j)
-            ref = pq.at[k, t, xh]
-            ref[...] = add(ref, rxq.at[k, t]).astype(BF16)
-            if j == 0:
-                send(("t1", k, 0), ref.at[:, :hr], r1q.at[k, 0], ynd)
-                send(("t1", k, 1), ref.at[:, hr:], r1q.at[k, 1], ypd)
-            if j == 1:
-                send(("t2", k, 0, 1), ref.at[:, hr:], r2q.at[k, 0, :, hr:], ynd)
-            if j == 2:
-                send(("t2", k, 1, 0), ref.at[:, :hr], r2q.at[k, 1, :, :hr], ypd)
+            send(("s2", k, way), ref, r2p.at[k, way, way], device)
+
+    def add_x(k, j, t):
+        arrive_groups(k, "qx", k, j)
+        ref = pq.at[k, t, xh]
+        ref[...] = add(ref, rxq.at[k, t]).astype(BF16)
+        return ref
+
+    def B1a(k):
+        ref = add_x(k, 0, yo)
+        send(("t1", k, 0), ref.at[:, :hr], r1q.at[k, 0], ynd)
+        send(("t1", k, 1), ref.at[:, hr:], r1q.at[k, 1], ypd)
+
+    def B1b(k):
+        ref = add_x(k, 1, yn)
+        send(("t2", k, 0, 1), ref.at[:, hr:], r2q.at[k, 0, :, hr:], ynd)
+        ref = add_x(k, 2, yp)
+        send(("t2", k, 1, 0), ref.at[:, :hr], r2q.at[k, 1, :, :hr], ypd)
 
     def B2(k):
         for way, t, device in ((0, yn, ynd), (1, yp, ypd)):
@@ -187,8 +202,8 @@
 
     def A2(k):
         for way in (0, 1):
-            for h in (0, 1):
-                arrive("s2", k, way, h)
+            arrive("s2", k, way)
+            arrive_groups(k, "s2i", k, way)
         ref = pp.at[k, y, oxh]
         ref[...] = add(ref, r2p.at[k, 0, oxh], r2p.at[k, 1, oxh]).astype(BF16)
         send(("rx", k), ref, rxp.at[k], x2)
@@ -205,22 +220,29 @@
         arrive("rx", k)
         activate(add(pp.at[k, y, xh], r2p.at[k, 0, xh], r2p.at[k, 1, xh], rxp.at[k]), dp.at[k, y, xh])
 
-    def A3s(k):
+    def A3x(k):
         ref = dp.at[k, y, xh]
         send(("dx", k), ref, ref, x2)
+
+    def A3y(k):
+        ref = dp.at[k, y, xh]
         send(("do", k, 0), ref, ref, ynd)
         send(("do", k, 1), ref, ref, ypd)
 
     def B3(k):
+        arrive_groups(k, "qx", k, 3)
         for way in (0, 1):
             for h in (0, 1):
                 arrive("t2", k, way, h)
-        activate(add(pq.at[k, y, xh], r2q.at[k, 0], r2q.at[k, 1]), dq.at[k, y, xh])
-
-    def B3s(k):
+        activate(add(pq.at[k, y, xh], rxq.at[k, y], r2q.at[k, 0], r2q.at[k, 1]), dq.at[k, y, xh])
+
+    def B3y(k):
         ref = dq.at[k, y, xh]
         send(("eo", k, 0), ref, ref, ynd)
         send(("eo", k, 1), ref, ref, ypd)
+
+    def B3x(k):
+        ref = dq.at[k, y, xh]
         send(("ex", k, 0), ref, ref, x2)
 
     def A4(k):
@@ -229,21 +251,25 @@
         send(("dt", k, 0), ref, ref, ynd)
         send(("dt", k, 1), ref, ref, ypd)
 
-    def A5(k):
+    def A5a(k):
         arrive("do", k, 0)
         ref = dp.at[k, yp, xh]
         send(("df", k, 0), ref, ref, ynd)
+
+    def A5b(k):
         arrive("dt", k, 1)
         ref = dp.at[k, yn, oxh]
         send(("df", k, 1), ref, ref, ypd)
 
-    def B4(k):
+    def B4y(k):
         arrive("eo", k, 0)
         ref = dq.at[k, yp, xh, :, :hr]
         send(("ef", k, 0), ref, ref, ynd)
         arrive("eo", k, 1)
         ref = dq.at[k, yn, xh, :, hr:]
         send(("ef", k, 1), ref, ref, ypd)
+
+    def B4x(k):
         for j, t in ((1, yp), (2, yn)):
             ref = dq.at[k, t, xh]
             send(("ex", k, j), ref, ref, x2)
@@ -277,7 +303,7 @@
 
         send(("igc", k), ig.at[k, :, oc], rigc.at[k], core)
 
-    def gradient(k, a, part, first, last):
+    def gradient(k, a, part, first, last, remote=False):
         left = ttr[a // 2, k, part, :]
         for ref, lanes in ((dp, slice(0, p_cols)), (dq, slice(p_cols, half))):
             right = ref[k, :, :, a].reshape(chunk, ref.shape[-1])
@@ -285,13 +311,16 @@
             if not first:
                 value += acc[a, part, lanes]
             if last:
-                go[a, part, lanes] = value.astype(BF16)
+                if remote:
+                    go[a, :, lanes] = value.astype(BF16)
+                else:
+                    lo = lanes.start
+                    outs[a][:, pl.ds(pl.multiple_of(c * half + lo, 128), lanes.stop - lo)] = value.astype(BF16)
             else:
                 acc[a, part, lanes] = value
 
-    outs = (gg_out, ug_out, dg_out)
-
     def G(k):
+        TR(k)
         first, last = k == 1, k == 0
         if not last:
             @pl.loop(0, 6)
@@ -300,11 +329,9 @@
         else:
             for h, remote in ((oc, True), (c, False)):
                 for a in range(3):
-                    gradient(k, a, frows(h), first, last)
+                    gradient(k, a, frows(h), first, last, remote)
                     if remote:
-                        send(("go", a), go.at[a, frows(h), :], outs[a].at[:, hcols(c)], core)
-                    else:
-                        bring(go.at[a, frows(h), :], outs[a].at[:, hcols(c)])
+                        send(("go", a), go.at[a], outs[a].at[:, hcols(c)], core)
 
     def both(k, h):
         return ig[k, h, c].astype(F32) + rigc[k, h].astype(F32)
@@ -344,20 +371,17 @@
     def I0f(_):
         for j in range(3):
             arrive("ix", j)
-        igo[:, cols(xh)] = (ig[0, xh, c, xl].astype(F32) + rix[0].astype(F32)).astype(BF16)
-        igo[:, cols(oxh)] = (rix[1].astype(F32) + rix[2].astype(F32)).astype(BF16)
-        bring(igo, ig_out)
+        ig_out[:, cols(xh)] = (ig[0, xh, c, xl].astype(F32) + rix[0].astype(F32)).astype(BF16)
+        ig_out[:, cols(oxh)] = (rix[1].astype(F32) + rix[2].astype(F32)).astype(BF16)
 
     steps = dict(
-        T1=T1, T2=T2, T3=T3, F=F, A1=A1, B1=B1, B2=B2, A2=A2, A3=A3, A3s=A3s, B3=B3, B3s=B3s, A4=A4, A5=A5, B4=B4,
-        B5=B5, TR=TR, C=C, G=G, I3=I3, I12=I12, I12b=I12b, I0=I0, I0f=I0f,
+        T1=T1, T2=T2, T3=T3, F=F, A1=A1, B1a=B1a, B1b=B1b, B2=B2, A2=A2, A3=A3, A3x=A3x, A3y=A3y, B3=B3, B3x=B3x,
+        B3y=B3y, A4=A4, A5a=A5a, A5b=A5b, B4x=B4x, B4y=B4y, B5=B5, C=C, G=G, I3=I3, I12=I12, I12b=I12b, I0=I0, I0f=I0f,
     )
-    for step, k in ORDER:
-        steps[step](k)
+    for step, *k in ORDER:
+        steps[step](*k)
     for a in range(3):
         arrive("go", a)
-    for cp in local[5:]:
-        cp.wait()
     for cp in all_sends:
         cp.wait_send()
     assert not arrivals, "left over"
@@ -375,9 +399,9 @@
     out_shapes = [tokens, gate_weight, up_weight, down_weight]
     return pl.pallas_call(
         kernel,
-        out_shape=[jax.ShapeDtypeStruct(o.shape, BF16) for o in out_shapes],
+        out_shape=[pltpu.VMEM(o.shape, BF16) for o in out_shapes],
         in_specs=[any_spec] * 5,
-        out_specs=[any_spec] * 4,
+        out_specs=[pl.BlockSpec(memory_space=pltpu.VMEM)] * 4,
         scratch_shapes=[
             vmem(3, feats, half),
             vmem(4, 2, 2, 2, 2, rows, feats),
@@ -393,19 +417,18 @@
             vmem(4, 4, 2, 3, rows, p_cols),
             vmem(4, 4, 2, 3, rows, q_cols),
             pltpu.VMEM((3, feats, half), F32),
-            vmem(3, feats, half),
+            vmem(3, own_f, half),
             vmem(4, 2, 2, 2, rows, feats),
             vmem(4, 2, 2, rows, feats),
             vmem(2, 2, rows, feats),
             vmem(2, 2, 2, rows, feats),
             vmem(3, rows, feats),
-            vmem(rows, model),
             pltpu.SemaphoreType.DMA((N_SEM,)),
             pltpu.SemaphoreType.DMA((N_SEM,)),
             pltpu.SemaphoreType.DMA((16,)),
         ],
         compiler_params=pltpu.CompilerParams(
-            collective_id=0, has_side_effects=True, vmem_limit_bytes=60 * 2**20
+            collective_id=0, has_side_effects=True, vmem_limit_bytes=52 * 2**20
         ),
         cost_estimate=pl.CostEstimate(flops=15 * 10**9, bytes_accessed=12 * 2**20, transcendentals=10**6),
     )(tokens, out_grad, gate_weight, up_weight, down_weight)

time: 126 us -> 112 us (0.89)
  Pallas kernels: 117 us -> 107 us
  local copies, waits for them, and re-layouts: 7.94 us -> 4.34 us
    pallas_call x1, Pallas kernels: 117 us -> 107 us  [on_device(): pl.pallas_call(kernel, out_shape=[pltpu.VMEM(o.shape, BF16) for o in out_...]
    unnamed x8 -> x4, local copies, waits for them, and re-layouts: 7.94 us -> 4.34 us
where the time goes in v2:
time: 112 us
  Pallas kernels  107 us (96%)
  local copies, waits for them, and re-layouts  4.34 us (4%)
    pallas_call x1, Pallas kernels, on_device(): pl.pallas_call(kernel, out_shape=[pltpu.VMEM(o.shape, BF16) for o in out_...  107 us
    unnamed x4, local copies, waits for them, and re-layouts  4.34 us

profile of v2, /device:TPU:1, one launch (start us, length us, event | category | flops | bytes accessed | tf_op | source)
XLA Modules:
  0.0 112.0 jit_solution(1990328355461096163)
XLA Ops:
  0.6 107.0 %shard_map.84 = (bf16[32,2048]{1,0:T(8,128)(2,1)S(1)}, bf16[512,1792]{1,0:T(8,128)(2,1)S(1)}, bf16[512,1792]{1,0:T(8,128)(2,1)S(1)}, bf16[512,1792]{1,0:T(8,128)(2,1)S(1)}) custom-call(bf16[32,2048]{1,0:T(8,128)(2,1)} %tok_in.1, bf16[32,2048]{1,0:T(8,128)(2,1)} %og_in.1, bf16[512,1792]{1,0:T(8,128)(2,1)} %wg_in.1, bf16[512,1792]{1,0:T(8,128)(2,1)} %wu_in.1, ...), custom_call_target="tpu_custom_call" | custom-call | flops 15000000512 | bytes 12582912 | tf_op jit(solution)/shard_map/pallas_call | solution.py:400
  107.7 0.7 copy.13
  108.3 1.2 %copy.14 = bf16[512,1792]{1,0:T(8,128)(2,1)} copy(bf16[512,1792]{1,0:T(8,128)(2,1)S(1)} %get-tuple-element.5) | data formatting | bytes 3670016
  109.6 1.2 %copy.15 = bf16[512,1792]{1,0:T(8,128)(2,1)} copy(bf16[512,1792]{1,0:T(8,128)(2,1)S(1)} %get-tuple-element.6) | data formatting | bytes 3670016
  110.8 1.2 %copy.16 = bf16[512,1792]{1,0:T(8,128)(2,1)} copy(bf16[512,1792]{1,0:T(8,128)(2,1)S(1)} %get-tuple-element.7) | data formatting | bytes 3670016

commit v3 on v2

--- a/solution.py
+++ b/solution.py
@@ -10,19 +10,22 @@
 BF16 = jnp.bfloat16
 F32 = jnp.float32
 MESH = pl.DeviceIdType.MESH
-N_SEM = 208
+N_SEM = 240
+PIECES = 4
 
 ORDER = (
-    ("T1", 0), ("F", 0, 0), ("T1", 1), ("F", 0, 1), ("A1", 0), ("T2", 0), ("B1a", 0), ("B1b", 0), ("F", 1),
-    ("F", 2), ("A1", 1), ("T3", 0), ("B1a", 1), ("F", 3), ("A2", 1), ("B1b", 1), ("B2", 1), ("B1a", 2), ("A1", 3),
-    ("B1b", 2), ("B2", 2), ("A2", 0), ("A1", 2), ("B2", 0), ("B3", 1), ("A2", 3), ("B1a", 3), ("B3y", 1),
-    ("B1b", 3), ("A3", 1), ("A3x", 1), ("A2", 2), ("B2", 3), ("B3x", 1), ("A3", 0), ("A3y", 1), ("A3", 3),
-    ("A3y", 3), ("B3", 2), ("A3x", 3), ("B4y", 1), ("B3", 3), ("A3", 2), ("B4x", 1), ("B3x", 3), ("B3y", 2),
-    ("A4", 1), ("B3y", 3), ("A4", 3), ("B5", 1), ("A5b", 1), ("B4y", 2), ("A3x", 2), ("A5a", 1), ("B4x", 2),
-    ("B4y", 3), ("A3y", 2), ("B4x", 3), ("A4", 2), ("A5a", 3), ("B5", 3), ("A3x", 0), ("B3", 0), ("A5b", 3),
-    ("B5", 2), ("B3y", 0), ("C", 1), ("B3x", 2), ("B3x", 0), ("G", 1), ("A5b", 2), ("A5a", 2), ("A3y", 0), ("C", 3),
-    ("B4y", 0), ("A4", 0), ("G", 3), ("I3", 0), ("B4x", 0), ("C", 2), ("A5a", 0), ("I12", 0), ("B5", 0), ("A5b", 0),
-    ("I12b", 0), ("G", 2), ("C", 0), ("I0", 0), ("G", 0), ("I0f", 0),
+    ("R", 0), ("Z", 0), ("F", 0, 0), ("R", 1), ("F", 0, 1), ("Z", 1), ("F", 0, 2), ("T2", 0), ("A1", 0),
+    ("F", 2, 0), ("T2", 1), ("F", 1, 0), ("F", 1, 1), ("F", 2, 1), ("T3", 0), ("B1a", 0), ("A1", 1), ("F", 3),
+    ("A2", 1), ("A1", 2), ("A1", 3), ("B1a", 1), ("B1a", 3), ("B1b", 1), ("B1b", 3), ("A2", 2), ("A2", 3),
+    ("B1a", 2), ("B2", 1), ("A3", 1), ("A3y", 1), ("A3x", 1), ("A3", 2), ("B1b", 2), ("B3", 1), ("B2", 3),
+    ("B3y", 1), ("A3x", 2), ("B1b", 0), ("B2", 2), ("A2", 0), ("A3", 3), ("B3", 3), ("B3y", 3), ("A4", 1),
+    ("A3x", 3), ("B4y", 1), ("B4x", 1), ("B3x", 1), ("B2", 0), ("B4y", 3), ("B3x", 3), ("A3y", 2), ("A5b", 1),
+    ("B3", 2), ("B3y", 2), ("B3x", 2), ("A5a", 1), ("A3y", 3), ("B5", 1), ("B4x", 3), ("B5", 3), ("A3", 0),
+    ("A3x", 0), ("A4", 3), ("A4", 2), ("B4y", 2), ("G", 1), ("C", 1, 0), ("B4x", 2), ("A5b", 3), ("A5a", 3),
+    ("B3", 0), ("A5b", 2), ("A5a", 2), ("B5", 2), ("B3y", 0), ("A3y", 0), ("C", 3, 0), ("C", 3, 1), ("A4", 0),
+    ("C", 1, 1), ("I3", 0), ("B3x", 0), ("C", 2, 0), ("B4y", 0), ("C", 2, 1), ("B4x", 0), ("I12", 0), ("A5a", 0),
+    ("G", 2), ("A5b", 0), ("B5", 0), ("I12b", 0), ("G", 3), ("C", 0, 0), ("C", 0, 1), ("I0", 0), ("Gr", 0),
+    ("Gl", 0), ("I0", 1), ("Gr", 1), ("Gr", 2), ("Gl", 1), ("Gl", 2), ("I0f", 0),
 )
 
 
@@ -51,7 +54,7 @@
     hcols = lambda h: pl.ds(pl.multiple_of(h * half, 128), half)
     frows = lambda h: pl.ds(pl.multiple_of(h * own_f, 16), own_f)
 
-    arrivals, all_sends = {}, []
+    arrivals, all_sends, ready = {}, [], []
 
     def send(name, src, dst, device):
         i = len(all_sends)
@@ -86,7 +89,7 @@
         pl.semaphore_signal(barrier, inc=1, device_id=device, device_id_type=MESH)
     pl.semaphore_wait(barrier, 8)
 
-    near = (("xlp", xlp, xh, xh, oxl), ("diag", diag, oxh, oxh, oxl), ("x2", x2, oxh, oxh, xl))
+    near = (("x2", x2, oxh, oxh, xl), ("xlp", xlp, xh, xh, oxl), ("diag", diag, oxh, oxh, oxl))
     for a in (0, 1):
         for name, device, h, _, _ in near:
             send(("x0", name, a), acts[a].at[:, cols(h)], tok.at[0, xh, c, xl, a], device)
@@ -100,27 +103,31 @@
         send(("zn", "own", a), mine, tok.at[2, xh, c, xl, a], zn)
         send(("zp", "own", a), mine, tok.at[1, xh, c, xl, a], zp)
 
-    def T1(a):
+    def R(a):
         for name, _, _, sxh, sxl in near:
             arrive("x0", name, a)
             block = tok.at[0, sxh, c, sxl, a]
             send(("c0", name, a), block, block, core)
+
+    def Z(a):
+        for name, _, _, sxh, sxl in near:
+            block = tok.at[0, sxh, c, sxl, a]
             send(("zn", name, a), block, tok.at[2, sxh, c, sxl, a], zn)
             send(("zp", name, a), block, tok.at[1, sxh, c, sxl, a], zp)
 
-    def T2(_):
+    def T2(a):
         for way in ("zn", "zp"):
             for name in ("own", "xlp", "diag", "x2"):
-                for a in (0, 1):
-                    arrive(way, name, a)
-        send(("zf", 0), tok.at[2, 0, c], tok.at[3, 0, c], zn)
-        send(("zf", 1), tok.at[1, 1, c], tok.at[3, 1, c], zp)
+                arrive(way, name, a)
+        send(("zf", 0, a), tok.at[2, 0, c, :, a], tok.at[3, 0, c, :, a], zn)
+        send(("zf", 1, a), tok.at[1, 1, c, :, a], tok.at[3, 1, c, :, a], zp)
         for k in (1, 2):
-            send(("ck", k), tok.at[k, :, c], tok.at[k, :, c], core)
+            send(("ck", k, a), tok.at[k, :, c, :, a], tok.at[k, :, c, :, a], core)
 
     def T3(_):
         for h in (0, 1):
-            arrive("zf", h)
+            for a in (0, 1):
+                arrive("zf", h, a)
             send(("ck3", h), tok.at[3, h, c], tok.at[3, h, c], core)
 
     def project(k, a):
@@ -129,22 +136,25 @@
         pq[k, :, :, a] = jnp.dot(left, w[a, :, p_cols:], preferred_element_type=F32).astype(BF16).reshape(4, 2, rows, q_cols)
 
     def groups(k):
-        return ((0, 2), (2, 3)) if k == 0 else ((0, 3),)
+        return (((0, 1), (1, 2), (2, 3)), ((0, 2), (2, 3)), ((0, 2), (2, 3)), ((0, 3),))[k]
 
     def F(k, g=0):
         first, last = groups(k)[g]
+        new = [a for a in (0, 1) if first <= 2 * a < last]
+        for a in new if k < 3 else ():
+            if k == 0:
+                local[a].wait()
+                for name in ("own", "xlp", "diag", "x2"):
+                    arrive("c0", name, a)
+            else:
+                arrive("ck", k, a)
         if k == 0:
-            local[g].wait()
-            for name in ("own", "xlp", "diag", "x2"):
-                arrive("c0", name, g)
             for a in range(first, last):
                 local[2 + a].wait()
                 arrive("w", a)
-        elif k == 3:
+        if k == 3:
             arrive("ck3", 0)
             arrive("ck3", 1)
-        else:
-            arrive("ck", k)
 
         @pl.loop(first, last)
         def _(a):
@@ -285,23 +295,23 @@
         def _(a):
             ttr[a, k] = tok[k, :, :, :, a].reshape(chunk, feats).T
 
-    def C(k):
-        for name in (("df", k, 0), ("df", k, 1), ("dt", k, 0), ("do", k, 1), ("ex", k, 0), ("ex", k, 1), ("ex", k, 2), ("ex", k, 3)):
-            arrive(*name)
+    def whole(k):
+        for name in [("df", k, 0), ("df", k, 1), ("dt", k, 0), ("do", k, 1)] + [("ex", k, n) for n in range(4)]:
+            if name in arrivals:
+                arrive(*name)
+
+    def C(k, j):
+        whole(k)
         nt = (((1,), (1,)), ((), ()))
-
-        @pl.loop(0, 2)
-        def _(j):
-            fr = pl.ds(pl.multiple_of(j * own_f, 128), own_f)
-            total = jnp.zeros((chunk, own_f), F32)
-            for a in (0, 1):
-                left = dp[k, :, :, a].reshape(chunk, p_cols)
-                total += lax.dot_general(left, w[a, fr, :p_cols], nt, preferred_element_type=F32)
-                left = dq[k, :, :, a].reshape(chunk, q_cols)
-                total += lax.dot_general(left, w[a, fr, p_cols:], nt, preferred_element_type=F32)
-            ig[k, :, :, :, :, fr] = total.astype(BF16).reshape(2, 2, 2, rows, own_f)
-
-        send(("igc", k), ig.at[k, :, oc], rigc.at[k], core)
+        fr = slice(j * own_f, (j + 1) * own_f)
+        total = jnp.zeros((chunk, own_f), F32)
+        for a in (0, 1):
+            left = dp[k, :, :, a].reshape(chunk, p_cols)
+            total += lax.dot_general(left, w[a, fr, :p_cols], nt, preferred_element_type=F32)
+            left = dq[k, :, :, a].reshape(chunk, q_cols)
+            total += lax.dot_general(left, w[a, fr, p_cols:], nt, preferred_element_type=F32)
+        ig[k, :, :, :, :, fr] = total.astype(BF16).reshape(2, 2, 2, rows, own_f)
+        send(("igc", k, j), ig.at[k, :, oc, :, :, fr], rigc.at[k, :, :, :, fr], core)
 
     def gradient(k, a, part, first, last, remote=False):
         left = ttr[a // 2, k, part, :]
@@ -320,24 +330,34 @@
                 acc[a, part, lanes] = value
 
     def G(k):
+        whole(k)
         TR(k)
-        first, last = k == 1, k == 0
-        if not last:
-            @pl.loop(0, 6)
-            def _(i):
-                gradient(k, i // 2, pl.ds(pl.multiple_of((i % 2) * own_f, 128), own_f), first, last)
-        else:
-            for h, remote in ((oc, True), (c, False)):
-                for a in range(3):
-                    gradient(k, a, frows(h), first, last, remote)
-                    if remote:
-                        send(("go", a), go.at[a], outs[a].at[:, hcols(c)], core)
+
+        @pl.loop(0, 6)
+        def _(i):
+            gradient(k, i // 2, pl.ds(pl.multiple_of((i % 2) * own_f, 128), own_f), k == 1, False)
+
+    def last_chunk():
+        whole(0)
+        if not ready:
+            ready.append(0)
+            TR(0)
+
+    def Gr(a):
+        last_chunk()
+        gradient(0, a, frows(oc), False, True, True)
+        send(("go", a), go.at[a], outs[a].at[:, hcols(c)], core)
+
+    def Gl(a):
+        last_chunk()
+        gradient(0, a, frows(c), False, True)
 
     def both(k, h):
         return ig[k, h, c].astype(F32) + rigc[k, h].astype(F32)
 
     def I3(_):
-        arrive("igc", 3)
+        arrive("igc", 3, 0)
+        arrive("igc", 3, 1)
         for h in (0, 1):
             ref = ig.at[3, h, c]
             ref[...] = both(3, h).astype(BF16)
@@ -345,7 +365,8 @@
 
     def I12(_):
         for k, device, way in ((1, zn, 0), (2, zp, 1)):
-            arrive("igc", k)
+            arrive("igc", k, 0)
+            arrive("igc", k, 1)
             h = 1 - way
             ref = ig.at[k, h, c]
             ref[...] = both(k, h).astype(BF16)
@@ -358,25 +379,31 @@
             ref[...] = (both(k, way) + rz1[way].astype(F32)).astype(BF16)
             send(("z2", way, way), ref, rz2.at[way, way], device)
 
-    def I0(_):
-        arrive("igc", 0)
+    def I0(j):
+        arrive("igc", 0, j)
+        fr = slice(j * own_f, (j + 1) * own_f)
         for h in (0, 1):
-            for way in (0, 1):
-                arrive("z2", way, h)
-            ig[0, h, c] = (both(0, h) + rz2[0, h].astype(F32) + rz2[1, h].astype(F32)).astype(BF16)
-        send(("ix", 0), ig.at[0, xh, c, oxl], rix.at[0], xlp)
-        send(("ix", 1), ig.at[0, oxh, c, oxl], rix.at[1], diag)
-        send(("ix", 2), ig.at[0, oxh, c, xl], rix.at[2], x2)
+            if j == 0:
+                for way in (0, 1):
+                    arrive("z2", way, h)
+            total = ig[0, h, c, :, :, fr].astype(F32) + rigc[0, h, :, :, fr].astype(F32)
+            total += rz2[0, h, :, :, fr].astype(F32) + rz2[1, h, :, :, fr].astype(F32)
+            ig[0, h, c, :, :, fr] = total.astype(BF16)
+        send(("ix", 2, j), ig.at[0, oxh, c, xl, :, fr], rix.at[2, :, fr], x2)
+        send(("ix", 0, j), ig.at[0, xh, c, oxl, :, fr], rix.at[0, :, fr], xlp)
+        send(("ix", 1, j), ig.at[0, oxh, c, oxl, :, fr], rix.at[1, :, fr], diag)
 
     def I0f(_):
-        for j in range(3):
-            arrive("ix", j)
+        for j in (0, 1):
+            for n in range(3):
+                arrive("ix", n, j)
         ig_out[:, cols(xh)] = (ig[0, xh, c, xl].astype(F32) + rix[0].astype(F32)).astype(BF16)
         ig_out[:, cols(oxh)] = (rix[1].astype(F32) + rix[2].astype(F32)).astype(BF16)
 
     steps = dict(
-        T1=T1, T2=T2, T3=T3, F=F, A1=A1, B1a=B1a, B1b=B1b, B2=B2, A2=A2, A3=A3, A3x=A3x, A3y=A3y, B3=B3, B3x=B3x,
-        B3y=B3y, A4=A4, A5a=A5a, A5b=A5b, B4x=B4x, B4y=B4y, B5=B5, C=C, G=G, I3=I3, I12=I12, I12b=I12b, I0=I0, I0f=I0f,
+        R=R, Z=Z, T2=T2, T3=T3, F=F, A1=A1, B1a=B1a, B1b=B1b, B2=B2, A2=A2, A3=A3, A3x=A3x, A3y=A3y, B3=B3, B3x=B3x,
+        B3y=B3y, A4=A4, A5a=A5a, A5b=A5b, B4x=B4x, B4y=B4y, B5=B5, C=C, G=G, Gr=Gr, Gl=Gl, I3=I3, I12=I12, I12b=I12b,
+        I0=I0, I0f=I0f,
     )
     for step, *k in ORDER:
         steps[step](*k)
@@ -385,6 +412,20 @@
     for cp in all_sends:
         cp.wait_send()
     assert not arrivals, "left over"
+
+
+def write_out(a, b, c, d, ao, bo, co, do, sem):
+    copies = []
+    for i, (src, dst) in enumerate(((b, bo), (c, co), (d, do), (a, ao))):
+        n = PIECES if src.shape[0] >= 16 * PIECES else 1
+        step = src.shape[0] // n
+        for j in range(n):
+            part = pl.ds(j * step, step)
+            cp = pltpu.make_async_copy(src.at[part], dst.at[part], sem.at[i, j])
+            cp.start()
+            copies.append(cp)
+    for cp in copies:
+        cp.wait()
 
 
 def on_device(tokens, out_grad, gate_weight, up_weight, down_weight):
@@ -397,7 +438,7 @@
     vmem = lambda *shape: pltpu.VMEM(shape, BF16)
     any_spec = pl.BlockSpec(memory_space=pl.ANY)
     out_shapes = [tokens, gate_weight, up_weight, down_weight]
-    return pl.pallas_call(
+    grads = pl.pallas_call(
         kernel,
         out_shape=[pltpu.VMEM(o.shape, BF16) for o in out_shapes],
         in_specs=[any_spec] * 5,
@@ -432,6 +473,15 @@
         ),
         cost_estimate=pl.CostEstimate(flops=15 * 10**9, bytes_accessed=12 * 2**20, transcendentals=10**6),
     )(tokens, out_grad, gate_weight, up_weight, down_weight)
+    return pl.pallas_call(
+        write_out,
+        out_shape=[jax.ShapeDtypeStruct(o.shape, BF16) for o in out_shapes],
+        in_specs=[any_spec] * 4,
+        out_specs=[any_spec] * 4,
+        scratch_shapes=[pltpu.SemaphoreType.DMA((4, PIECES))],
+        compiler_params=pltpu.CompilerParams(vmem_limit_bytes=2 * 2**20),
+        cost_estimate=pl.CostEstimate(flops=0, bytes_accessed=12 * 2**20, transcendentals=0),
+    )(*grads)
 
 
 def solution(mesh):

time: 112 us -> 109 us (0.973)
  local copies, waits for them, and re-layouts: 4.34 us -> 0 us
    unnamed x4 -> x0, local copies, waits for them, and re-layouts: 4.34 us -> none
    pallas_call x0 -> x1, Pallas kernels: none -> 2.58 us  [on_device(): pl.pallas_call(write_out, out_shape=[jax.ShapeDtypeStruct(o.shape, BF16)...]
    pallas_call x1, Pallas kernels: 107 us -> 105 us  [on_device(): pl.pallas_call(kernel, out_shape=[pltpu.VMEM(o.shape, BF16) for o in out_...]
where the time goes in v3:
time: 109 us
  Pallas kernels  108 us (99%)
    pallas_call x1, Pallas kernels, on_device(): pl.pallas_call(kernel, out_shape=[pltpu.VMEM(o.shape, BF16) for o in out_...  105 us
    pallas_call x1, Pallas kernels, on_device(): pl.pallas_call(write_out, out_shape=[jax.ShapeDtypeStruct(o.shape, BF16)...  2.58 us

profile of v3, /device:TPU:1, one launch (start us, length us, event | category | flops | bytes accessed | tf_op | source)
XLA Modules:
  0.0 108.5 jit_solution(595818459028683688)
XLA Ops:
  0.6 105.1 %shard_map.84 = (bf16[32,2048]{1,0:T(8,128)(2,1)S(1)}, bf16[512,1792]{1,0:T(8,128)(2,1)S(1)}, bf16[512,1792]{1,0:T(8,128)(2,1)S(1)}, bf16[512,1792]{1,0:T(8,128)(2,1)S(1)}) custom-call(bf16[32,2048]{1,0:T(8,128)(2,1)} %tok_in.1, bf16[32,2048]{1,0:T(8,128)(2,1)} %og_in.1, bf16[512,1792]{1,0:T(8,128)(2,1)} %wg_in.1, bf16[512,1792]{1,0:T(8,128)(2,1)} %wu_in.1, ...), custom_call_target="tpu_custom_call" | custom-call | flops 15000000512 | bytes 12582912 | tf_op jit(solution)/shard_map/pallas_call | solution.py:441
  105.8 2.6 %shard_map.85 = (bf16[32,2048]{1,0:T(8,128)(2,1)}, bf16[512,1792]{1,0:T(8,128)(2,1)}, bf16[512,1792]{1,0:T(8,128)(2,1)}, bf16[512,1792]{1,0:T(8,128)(2,1)}) custom-call(bf16[32,2048]{1,0:T(8,128)(2,1)S(1)} %get-tuple-element.8.a, bf16[512,1792]{1,0:T(8,128)(2,1)S(1)} %get-tuple-element.9.b, bf16[512,1792]{1,0:T(8,128)(2,1)S(1)} %get-tuple-element.10.c, ...), custom_call_target="tpu_custom_call" | custom-call | bytes 12582912 | tf_op jit(solution)/shard_map/pallas_call | solution.py:476

commit v4 on v3

--- a/solution.py
+++ b/solution.py
@@ -10,28 +10,32 @@
 BF16 = jnp.bfloat16
 F32 = jnp.float32
 MESH = pl.DeviceIdType.MESH
-N_SEM = 240
+N_SEM = 272
 PIECES = 4
 
 ORDER = (
     ("R", 0), ("Z", 0), ("F", 0, 0), ("R", 1), ("F", 0, 1), ("Z", 1), ("F", 0, 2), ("T2", 0), ("A1", 0),
-    ("F", 2, 0), ("T2", 1), ("F", 1, 0), ("F", 1, 1), ("F", 2, 1), ("T3", 0), ("B1a", 0), ("A1", 1), ("F", 3),
-    ("A2", 1), ("A1", 2), ("A1", 3), ("B1a", 1), ("B1a", 3), ("B1b", 1), ("B1b", 3), ("A2", 2), ("A2", 3),
-    ("B1a", 2), ("B2", 1), ("A3", 1), ("A3y", 1), ("A3x", 1), ("A3", 2), ("B1b", 2), ("B3", 1), ("B2", 3),
-    ("B3y", 1), ("A3x", 2), ("B1b", 0), ("B2", 2), ("A2", 0), ("A3", 3), ("B3", 3), ("B3y", 3), ("A4", 1),
-    ("A3x", 3), ("B4y", 1), ("B4x", 1), ("B3x", 1), ("B2", 0), ("B4y", 3), ("B3x", 3), ("A3y", 2), ("A5b", 1),
-    ("B3", 2), ("B3y", 2), ("B3x", 2), ("A5a", 1), ("A3y", 3), ("B5", 1), ("B4x", 3), ("B5", 3), ("A3", 0),
-    ("A3x", 0), ("A4", 3), ("A4", 2), ("B4y", 2), ("G", 1), ("C", 1, 0), ("B4x", 2), ("A5b", 3), ("A5a", 3),
-    ("B3", 0), ("A5b", 2), ("A5a", 2), ("B5", 2), ("B3y", 0), ("A3y", 0), ("C", 3, 0), ("C", 3, 1), ("A4", 0),
-    ("C", 1, 1), ("I3", 0), ("B3x", 0), ("C", 2, 0), ("B4y", 0), ("C", 2, 1), ("B4x", 0), ("I12", 0), ("A5a", 0),
-    ("G", 2), ("A5b", 0), ("B5", 0), ("I12b", 0), ("G", 3), ("C", 0, 0), ("C", 0, 1), ("I0", 0), ("Gr", 0),
-    ("Gl", 0), ("I0", 1), ("Gr", 1), ("Gr", 2), ("Gl", 1), ("Gl", 2), ("I0f", 0),
+    ("F", 1, 0), ("B1a", 0), ("T2", 1), ("F", 1, 1), ("F", 2, 0), ("F", 2, 1), ("T3", 0), ("A1", 1), ("F", 3),
+    ("B1a", 2), ("B1a", 1), ("B1b", 2), ("A1", 2), ("B1a", 3), ("A1", 3), ("A2", 1), ("B2", 2), ("B1b", 1),
+    ("B1b", 0), ("A2", 0), ("A2", 2), ("B1b", 3), ("A3", 1), ("A2", 3), ("A3x", 1, 0), ("B2", 1), ("A3", 0),
+    ("B2", 0), ("B2", 3), ("B3", 2), ("B3y", 2, 0), ("A3x", 0, 0), ("B3x", 2, 0), ("A3y", 1, 0), ("B3", 1),
+    ("A3", 3), ("B3", 3), ("B3x", 3, 0), ("B3y", 1, 0), ("B3y", 3, 0), ("A3x", 3, 0), ("A4", 1, 0), ("A3", 2),
+    ("A3x", 2, 0), ("B4y", 1, 0), ("A5a", 1, 0), ("B4y", 3, 0), ("B4x", 1, 0), ("A3y", 3, 0), ("B5", 1, 0),
+    ("B3x", 1, 0), ("B4y", 2, 0), ("A5b", 1, 0), ("B3", 0), ("A4", 3, 0), ("A3y", 2, 0), ("B4x", 3, 0),
+    ("A5a", 3, 0), ("B5", 3, 0), ("A4", 2, 0), ("C", 1, 0), ("B5", 2, 0), ("G", 1, 2), ("A5b", 3, 0), ("A5a", 2, 0),
+    ("B4x", 2, 0), ("A3x", 0, 1), ("C", 1, 1), ("G", 1, 0), ("A5b", 2, 0), ("B3y", 0, 0), ("A3y", 0, 0),
+    ("G", 1, 1), ("A4", 0, 0), ("C", 3, 0), ("C", 3, 1), ("G", 3, 2), ("I3", 0), ("C", 2, 0), ("C", 2, 1),
+    ("B3y", 0, 1), ("B4y", 0, 0), ("B4x", 0, 0), ("A3y", 0, 1), ("A4", 0, 1), ("A5a", 0, 0), ("I12", 0),
+    ("G", 2, 0), ("A5b", 0, 0), ("B3x", 0, 0), ("G", 3, 1), ("B5", 0, 0), ("I12b", 0), ("G", 3, 0), ("A5a", 0, 1),
+    ("B4y", 0, 1), ("A5b", 0, 1), ("G", 2, 1), ("Gp", 0), ("B4x", 0, 1), ("CP", 0), ("B3x", 0, 1), ("C", 0, 0),
+    ("C", 0, 1), ("B5", 0, 1), ("C", 0, 2), ("Gp", 1), ("I0", 0), ("C", 0, 3), ("I0", 1), ("I0", 2), ("Gr", 1),
+    ("Gl", 0), ("I0", 3), ("G", 2, 2), ("Gr", 0), ("Gp", 2), ("Gr", 2), ("Gl", 2), ("Gl", 1), ("I0f", 0),
 )
 
 
 def kernel(
     tok_in, og_in, wg_in, wu_in, wd_in, ig_out, gg_out, ug_out, dg_out,
-    w, tok, ttr, pp, pq, r1p, r1q, r2p, r2q, rxp, rxq, dp, dq, acc, go, ig, rigc, rz1, rz2, rix,
+    w, tok, ttr, pp, pq, r1p, r1q, r2p, r2q, rxp, rxq, dp, dq, acc, go, ig, rigc, rz1, rz2, rix, igp,
     ssem, rsem, lsem,
 ):
     inp, wt, y = lax.axis_index("inp"), lax.axis_index("wt"), lax.axis_index("out")
@@ -230,15 +234,6 @@
         arrive("rx", k)
         activate(add(pp.at[k, y, xh], r2p.at[k, 0, xh], r2p.at[k, 1, xh], rxp.at[k]), dp.at[k, y, xh])
 
-    def A3x(k):
-        ref = dp.at[k, y, xh]
-        send(("dx", k), ref, ref, x2)
-
-    def A3y(k):
-        ref = dp.at[k, y, xh]
-        send(("do", k, 0), ref, ref, ynd)
-        send(("do", k, 1), ref, ref, ypd)
-
     def B3(k):
         arrive_groups(k, "qx", k, 3)
         for way in (0, 1):
@@ -246,76 +241,106 @@
                 arrive("t2", k, way, h)
         activate(add(pq.at[k, y, xh], rxq.at[k, y], r2q.at[k, 0], r2q.at[k, 1]), dq.at[k, y, xh])
 
-    def B3y(k):
-        ref = dq.at[k, y, xh]
-        send(("eo", k, 0), ref, ref, ynd)
-        send(("eo", k, 1), ref, ref, ypd)
-
-    def B3x(k):
-        ref = dq.at[k, y, xh]
-        send(("ex", k, 0), ref, ref, x2)
-
-    def A4(k):
-        arrive("dx", k)
-        ref = dp.at[k, y, oxh]
-        send(("dt", k, 0), ref, ref, ynd)
-        send(("dt", k, 1), ref, ref, ypd)
-
-    def A5a(k):
-        arrive("do", k, 0)
-        ref = dp.at[k, yp, xh]
-        send(("df", k, 0), ref, ref, ynd)
-
-    def A5b(k):
-        arrive("dt", k, 1)
-        ref = dp.at[k, yn, oxh]
-        send(("df", k, 1), ref, ref, ypd)
-
-    def B4y(k):
-        arrive("eo", k, 0)
-        ref = dq.at[k, yp, xh, :, :hr]
-        send(("ef", k, 0), ref, ref, ynd)
-        arrive("eo", k, 1)
-        ref = dq.at[k, yn, xh, :, hr:]
-        send(("ef", k, 1), ref, ref, ypd)
-
-    def B4x(k):
+    def late(k, g):
+        return (slice(0, 2), slice(2, 3))[g] if k == 0 else slice(0, 3)
+
+    def A3x(k, g):
+        ref = dp.at[k, y, xh, late(k, g)]
+        send(("dx", k, g), ref, ref, x2)
+
+    def A3y(k, g):
+        ref = dp.at[k, y, xh, late(k, g)]
+        send(("do", k, 0, g), ref, ref, ynd)
+        send(("do", k, 1, g), ref, ref, ypd)
+
+    def B3y(k, g):
+        ref = dq.at[k, y, xh, late(k, g)]
+        send(("eo", k, 0, g), ref, ref, ynd)
+        send(("eo", k, 1, g), ref, ref, ypd)
+
+    def B3x(k, g):
+        ref = dq.at[k, y, xh, late(k, g)]
+        send(("ex", k, 0, g), ref, ref, x2)
+
+    def A4(k, g):
+        arrive("dx", k, g)
+        ref = dp.at[k, y, oxh, late(k, g)]
+        send(("dt", k, 0, g), ref, ref, ynd)
+        send(("dt", k, 1, g), ref, ref, ypd)
+
+    def A5a(k, g):
+        arrive("do", k, 0, g)
+        ref = dp.at[k, yp, xh, late(k, g)]
+        send(("df", k, 0, g), ref, ref, ynd)
+
+    def A5b(k, g):
+        arrive("dt", k, 1, g)
+        ref = dp.at[k, yn, oxh, late(k, g)]
+        send(("df", k, 1, g), ref, ref, ypd)
+
+    def B4y(k, g):
+        arrive("eo", k, 0, g)
+        ref = dq.at[k, yp, xh, late(k, g), :hr]
+        send(("ef", k, 0, g), ref, ref, ynd)
+        arrive("eo", k, 1, g)
+        ref = dq.at[k, yn, xh, late(k, g), hr:]
+        send(("ef", k, 1, g), ref, ref, ypd)
+
+    def B4x(k, g):
         for j, t in ((1, yp), (2, yn)):
-            ref = dq.at[k, t, xh]
-            send(("ex", k, j), ref, ref, x2)
-
-    def B5(k):
-        arrive("ef", k, 0)
-        arrive("ef", k, 1)
-        ref = dq.at[k, yo, xh]
-        send(("ex", k, 3), ref, ref, x2)
+            ref = dq.at[k, t, xh, late(k, g)]
+            send(("ex", k, j, g), ref, ref, x2)
+
+    def B5(k, g):
+        arrive("ef", k, 0, g)
+        arrive("ef", k, 1, g)
+        ref = dq.at[k, yo, xh, late(k, g)]
+        send(("ex", k, 3, g), ref, ref, x2)
 
     def TR(k):
         @pl.loop(0, 2)
         def _(a):
             ttr[a, k] = tok[k, :, :, :, a].reshape(chunk, feats).T
 
-    def whole(k):
-        for name in [("df", k, 0), ("df", k, 1), ("dt", k, 0), ("do", k, 1)] + [("ex", k, n) for n in range(4)]:
+    def whole_p(k, g=0):
+        for name in (("df", k, 0, g), ("df", k, 1, g), ("dt", k, 0, g), ("do", k, 1, g)):
             if name in arrivals:
                 arrive(*name)
 
+    def whole(k, g=0):
+        whole_p(k, g)
+        for n in range(4):
+            if ("ex", k, n, g) in arrivals:
+                arrive("ex", k, n, g)
+
+    def back(k, ref, fr, lanes):
+        total = None
+        for a in (0, 1):
+            left = ref[k, :, :, a].reshape(chunk, ref.shape[-1])
+            part = lax.dot_general(left, w[a, fr, lanes], (((1,), (1,)), ((), ())), preferred_element_type=F32)
+            total = part if total is None else total + part
+        return total
+
+    def pieces(k):
+        n = PIECES if k == 0 else 2
+        return [slice(j * (feats // n), (j + 1) * (feats // n)) for j in range(n)]
+
+    def CP(_):
+        whole_p(0)
+        for fr in pieces(1):
+            igp[:, fr] = back(0, dp, fr, slice(0, p_cols))
+
     def C(k, j):
         whole(k)
-        nt = (((1,), (1,)), ((), ()))
-        fr = slice(j * own_f, (j + 1) * own_f)
-        total = jnp.zeros((chunk, own_f), F32)
-        for a in (0, 1):
-            left = dp[k, :, :, a].reshape(chunk, p_cols)
-            total += lax.dot_general(left, w[a, fr, :p_cols], nt, preferred_element_type=F32)
-            left = dq[k, :, :, a].reshape(chunk, q_cols)
-            total += lax.dot_general(left, w[a, fr, p_cols:], nt, preferred_element_type=F32)
-        ig[k, :, :, :, :, fr] = total.astype(BF16).reshape(2, 2, 2, rows, own_f)
+        fr = pieces(k)[j]
+        total = back(k, dq, fr, slice(p_cols, half))
+        total += igp[:, fr] if k == 0 else back(k, dp, fr, slice(0, p_cols))
+        ig[k, :, :, :, :, fr] = total.astype(BF16).reshape(2, 2, 2, rows, total.shape[-1])
         send(("igc", k, j), ig.at[k, :, oc, :, :, fr], rigc.at[k, :, :, :, fr], core)
 
-    def gradient(k, a, part, first, last, remote=False):
+    def gradient(k, a, part, first, last, remote=False, sets=(0, 1)):
         left = ttr[a // 2, k, part, :]
-        for ref, lanes in ((dp, slice(0, p_cols)), (dq, slice(p_cols, half))):
+        for ref, lanes in [((dp, slice(0, p_cols)), (dq, slice(p_cols, half)))[n] for n in sets]:
             right = ref[k, :, :, a].reshape(chunk, ref.shape[-1])
             value = jnp.dot(left, right, preferred_element_type=F32)
             if not first:
@@ -329,28 +354,33 @@
             else:
                 acc[a, part, lanes] = value
 
-    def G(k):
+    def turned(k):
+        if k not in ready:
+            ready.append(k)
+            TR(k)
+
+    def G(k, a):
         whole(k)
-        TR(k)
-
-        @pl.loop(0, 6)
+        turned(k)
+
+        @pl.loop(0, 2)
         def _(i):
-            gradient(k, i // 2, pl.ds(pl.multiple_of((i % 2) * own_f, 128), own_f), k == 1, False)
-
-    def last_chunk():
-        whole(0)
-        if not ready:
-            ready.append(0)
-            TR(0)
+            gradient(k, a, pl.ds(pl.multiple_of(i * own_f, 128), own_f), k == 1, False)
+
+    def Gp(a):
+        whole_p(0, a // 2)
+        turned(0)
+        gradient(0, a, frows(oc), False, True, True, (0,))
+        gradient(0, a, frows(c), False, True, False, (0,))
 
     def Gr(a):
-        last_chunk()
-        gradient(0, a, frows(oc), False, True, True)
+        whole(0, a // 2)
+        gradient(0, a, frows(oc), False, True, True, (1,))
         send(("go", a), go.at[a], outs[a].at[:, hcols(c)], core)
 
     def Gl(a):
-        last_chunk()
-        gradient(0, a, frows(c), False, True)
+        whole(0, a // 2)
+        gradient(0, a, frows(c), False, True, False, (1,))
 
     def both(k, h):
         return ig[k, h, c].astype(F32) + rigc[k, h].astype(F32)
@@ -381,7 +411,7 @@
 
     def I0(j):
         arrive("igc", 0, j)
-        fr = slice(j * own_f, (j + 1) * own_f)
+        fr = pieces(0)[j]
         for h in (0, 1):
             if j == 0:
                 for way in (0, 1):
@@ -394,7 +424,7 @@
         send(("ix", 1, j), ig.at[0, oxh, c, oxl, :, fr], rix.at[1, :, fr], diag)
 
     def I0f(_):
-        for j in (0, 1):
+        for j in range(PIECES):
             for n in range(3):
                 arrive("ix", n, j)
         ig_out[:, cols(xh)] = (ig[0, xh, c, xl].astype(F32) + rix[0].astype(F32)).astype(BF16)
@@ -402,7 +432,7 @@
 
     steps = dict(
         R=R, Z=Z, T2=T2, T3=T3, F=F, A1=A1, B1a=B1a, B1b=B1b, B2=B2, A2=A2, A3=A3, A3x=A3x, A3y=A3y, B3=B3, B3x=B3x,
-        B3y=B3y, A4=A4, A5a=A5a, A5b=A5b, B4x=B4x, B4y=B4y, B5=B5, C=C, G=G, Gr=Gr, Gl=Gl, I3=I3, I12=I12, I12b=I12b,
+        B3y=B3y, A4=A4, A5a=A5a, A5b=A5b, B4x=B4x, B4y=B4y, B5=B5, CP=CP, C=C, G=G, Gp=Gp, Gr=Gr, Gl=Gl, I3=I3, I12=I12, I12b=I12b,
         I0=I0, I0f=I0f,
     )
     for step, *k in ORDER:
@@ -464,12 +494,13 @@
             vmem(2, 2, rows, feats),
             vmem(2, 2, 2, rows, feats),
             vmem(3, rows, feats),
+            pltpu.VMEM((8 * rows, feats), F32),
             pltpu.SemaphoreType.DMA((N_SEM,)),
             pltpu.SemaphoreType.DMA((N_SEM,)),
             pltpu.SemaphoreType.DMA((16,)),
         ],
         compiler_params=pltpu.CompilerParams(
-            collective_id=0, has_side_effects=True, vmem_limit_bytes=52 * 2**20
+            collective_id=0, has_side_effects=True, vmem_limit_bytes=54 * 2**20
         ),
         cost_estimate=pl.CostEstimate(flops=15 * 10**9, bytes_accessed=12 * 2**20, transcendentals=10**6),
     )(tokens, out_grad, gate_weight, up_weight, down_weight)

time: 109 us -> 109 us (level)
  no operation moved by 1% of the time
where the time goes in v4:
time: 109 us
  Pallas kernels  108 us (99%)
    pallas_call x1, Pallas kernels, on_device(): pl.pallas_call(kernel, out_shape=[pltpu.VMEM(o.shape, BF16) for o in out_...  105 us
    pallas_call x1, Pallas kernels, on_device(): pl.pallas_call(write_out, out_shape=[jax.ShapeDtypeStruct(o.shape, BF16)...  2.58 us

profile of v4, /device:TPU:1, one launch (start us, length us, event | category | flops | bytes accessed | tf_op | source)
XLA Modules:
  0.0 108.8 jit_solution(14793759025992868219)
XLA Ops:
  0.6 105.4 %shard_map.84 = (bf16[32,2048]{1,0:T(8,128)(2,1)S(1)}, bf16[512,1792]{1,0:T(8,128)(2,1)S(1)}, bf16[512,1792]{1,0:T(8,128)(2,1)S(1)}, bf16[512,1792]{1,0:T(8,128)(2,1)S(1)}) custom-call(bf16[32,2048]{1,0:T(8,128)(2,1)} %tok_in.1, bf16[32,2048]{1,0:T(8,128)(2,1)} %og_in.1, bf16[512,1792]{1,0:T(8,128)(2,1)} %wg_in.1, bf16[512,1792]{1,0:T(8,128)(2,1)} %wu_in.1, ...), custom_call_target="tpu_custom_call" | custom-call | flops 15000000512 | bytes 12582912 | tf_op jit(solution)/shard_map/pallas_call | solution.py:471
  106.0 2.6 %shard_map.85 = (bf16[32,2048]{1,0:T(8,128)(2,1)}, bf16[512,1792]{1,0:T(8,128)(2,1)}, bf16[512,1792]{1,0:T(8,128)(2,1)}, bf16[512,1792]{1,0:T(8,128)(2,1)}) custom-call(bf16[32,2048]{1,0:T(8,128)(2,1)S(1)} %get-tuple-element.8.a, bf16[512,1792]{1,0:T(8,128)(2,1)S(1)} %get-tuple-element.9.b, bf16[512,1792]{1,0:T(8,128)(2,1)S(1)} %get-tuple-element.10.c, ...), custom_call_target="tpu_custom_call" | custom-call | bytes 12582912 | tf_op jit(solution)/shard_map/pallas_call | solution.py:507
